TPU v7x, 128 devices: a whole 4x4x4 slice. The times are simulated.
128 devices in a mesh: seq: 32 (over x, z_hi, y), chan: 4 (over z_lo, core).
Axes of the slice: x: 4, y: 4, z: 4 (z_hi: 2, z_lo: 2; z = z_hi * 2 + z_lo), core: 2. Of those that a mesh axis runs over, the one named last changes fastest.
Arguments:
- layer_input: bfloat16 [4096, 16384], P('chan', 'seq'), may hold values from -6 to 6
- query_proj: bfloat16 [4096, 16384], P('chan', 'seq'), may hold values from -6 to 6
- key_proj: bfloat16 [4096, 16384], P('chan', 'seq'), may hold values from -6 to 6
- value_proj: bfloat16 [4096, 16384], P('chan', 'seq'), may hold values from -6 to 6
- filter_taps: float32 [8, 16384], P('chan', 'seq'), may hold values from -1 to 1
- grad_out: bfloat16 [4096, 16384], P('chan', 'seq'), may hold values from -6 to 6
Outputs:
- mixed_out: bfloat16 [4096, 16384], P('chan', 'seq')
- grad_query: bfloat16 [4096, 16384], P('chan', 'seq')
- grad_key: bfloat16 [4096, 16384], P('chan', 'seq')
- grad_value: bfloat16 [4096, 16384], P('chan', 'seq')
- filter_grad: float32 [8, 16384], P('chan', 'seq')
- weight_grad: float32 [4096, 4096], P('seq', 'chan')
All inputs are finite; a program needn't handle non-finite values.
Results may differ from a plain program's by a relative error of at most 0.0058.
Values may be sent and summed in bfloat16 or wider, within the bound.
A program may use at most 128 MiB of HBM per device.

v0:
```python
import math

import jax
import jax.numpy as jnp
from jax import lax
from jax.sharding import PartitionSpec as P

GROUP = 512


def factor_sizes(length):
    padded = 2 * length
    inner_size = math.gcd(length, 2 ** ((padded.bit_length() - 1) // 2))
    return (inner_size, padded // inner_size)


def dft_pair(extent, orient):
    indices = jnp.arange(extent, dtype=jnp.int32)
    phases = indices[:, None] * indices[None, :] % extent
    angles = 2.0 * math.pi / extent * phases.astype(jnp.float32)
    return (jnp.cos(angles), orient * jnp.sin(angles))


def twiddle_pair(outer_size, inner_size, orient):
    total_size = outer_size * inner_size
    outer_index = jnp.arange(outer_size, dtype=jnp.int32)
    inner_index = jnp.arange(inner_size, dtype=jnp.int32)
    phases = outer_index[:, None] * inner_index[None, :] % total_size
    angles = 2.0 * math.pi / total_size * phases.astype(jnp.float32)
    return (jnp.cos(angles), orient * jnp.sin(angles))


def contract(pattern, first_op, second_op):
    return jnp.einsum(
        pattern,
        first_op,
        second_op,
        precision=lax.Precision.HIGHEST,
        preferred_element_type=jnp.float32,
    )


def forward_transform(signal, inner_size, outer_size):
    extent = signal.shape[0]
    blocks = signal.reshape(extent, outer_size // 2, inner_size)
    outer_cos, outer_sin = dft_pair(outer_size, -1.0)
    half_cos = outer_cos[:, : outer_size // 2]
    half_sin = outer_sin[:, : outer_size // 2]
    real_part = contract("kt,pta->pka", half_cos, blocks)
    imag_part = contract("kt,pta->pka", half_sin, blocks)
    twist_cos, twist_sin = twiddle_pair(outer_size, inner_size, -1.0)
    real_twist = real_part * twist_cos - imag_part * twist_sin
    imag_twist = real_part * twist_sin + imag_part * twist_cos
    inner_cos, inner_sin = dft_pair(inner_size, -1.0)
    real_out = contract("pkt,tj->pkj", real_twist, inner_cos) - contract(
        "pkt,tj->pkj", imag_twist, inner_sin
    )
    imag_out = contract("pkt,tj->pkj", real_twist, inner_sin) + contract(
        "pkt,tj->pkj", imag_twist, inner_cos
    )
    return (real_out, imag_out)


def inverse_transform(real_in, imag_in, inner_size, outer_size):
    inner_cos, inner_sin = dft_pair(inner_size, 1.0)
    real_part = contract("pkj,jt->pkt", real_in, inner_cos) - contract(
        "pkj,jt->pkt", imag_in, inner_sin
    )
    imag_part = contract("pkj,jt->pkt", real_in, inner_sin) + contract(
        "pkj,jt->pkt", imag_in, inner_cos
    )
    twist_cos, twist_sin = twiddle_pair(outer_size, inner_size, 1.0)
    real_twist = real_part * twist_cos - imag_part * twist_sin
    imag_twist = real_part * twist_sin + imag_part * twist_cos
    outer_cos, outer_sin = dft_pair(outer_size, 1.0)
    half_cos = outer_cos[: outer_size // 2, :]
    half_sin = outer_sin[: outer_size // 2, :]
    signal = contract("tk,pka->pta", half_cos, real_twist) - contract(
        "tk,pka->pta", half_sin, imag_twist
    )
    extent = real_in.shape[0]
    return signal.reshape(extent, outer_size // 2 * inner_size) * (1.0 / (outer_size * inner_size))


def convolve(input_real, input_imag, taps_real, taps_imag, inner_size, outer_size):
    real_prod = taps_real * input_real - taps_imag * input_imag
    imag_prod = taps_real * input_imag + taps_imag * input_real
    return inverse_transform(real_prod, imag_prod, inner_size, outer_size).astype(jnp.bfloat16)


def correlate(
    up_real, up_imag, input_real, input_imag, taps_real, taps_imag, inner_size, outer_size, factor
):
    real_prod = taps_real * up_real + taps_imag * up_imag
    imag_prod = taps_real * up_imag - taps_imag * up_real
    back_long = inverse_transform(real_prod, imag_prod, inner_size, outer_size).astype(jnp.bfloat16)
    grad_real = jnp.sum(up_real * input_real + up_imag * input_imag, axis=0, keepdims=True)
    grad_imag = jnp.sum(up_imag * input_real - up_real * input_imag, axis=0, keepdims=True)
    taps_grad = inverse_transform(grad_real, grad_imag, inner_size, outer_size) * factor
    return (back_long, taps_grad)


def weight_sum(layer_input, grad_query, factor):
    gathered = lax.all_gather(layer_input, "chan", axis=0, tiled=True)
    summed = lax.psum_scatter(
        jnp.einsum("it,jt->ij", gathered, grad_query, preferred_element_type=jnp.float32),
        "seq",
        scatter_dimension=0,
        tiled=True,
    )
    return summed * factor


def per_device(layer_input, query_proj, key_proj, value_proj, filter_taps, grad_out):
    float_type = jnp.float32
    half_type = jnp.bfloat16
    seq_count = lax.axis_size("seq")
    tok_dev = query_proj.shape[1]
    length = seq_count * tok_dev
    channels = query_proj.shape[0]
    piece_size = channels // seq_count
    inner_size, outer_size = factor_sizes(length)
    weight_factor = 1.0 / math.sqrt(length)
    taps_factor = 1.0 / math.sqrt(GROUP * length)
    mixed_in = (key_proj.astype(float_type) * value_proj.astype(float_type)).astype(half_type)
    upstream = (grad_out.astype(float_type) * query_proj.astype(float_type)).astype(half_type)
    full_taps = lax.all_gather(filter_taps, "seq", axis=1, tiled=True)
    local_group = lax.axis_index("seq") * piece_size // GROUP
    taps_row = lax.dynamic_slice_in_dim(full_taps, local_group, 1, 0)
    taps_real, taps_imag = forward_transform(taps_row, inner_size, outer_size)
    signal = lax.all_to_all(mixed_in, "seq", split_axis=0, concat_axis=1, tiled=True)
    input_real, input_imag = forward_transform(signal.astype(float_type), inner_size, outer_size)
    conv_long = convolve(input_real, input_imag, taps_real, taps_imag, inner_size, outer_size)
    conv_out = lax.all_to_all(conv_long, "seq", split_axis=1, concat_axis=0, tiled=True)
    grad_query = (grad_out.astype(float_type) * conv_out.astype(float_type)).astype(half_type)
    back_signal = lax.all_to_all(upstream, "seq", split_axis=0, concat_axis=1, tiled=True)
    up_real, up_imag = forward_transform(back_signal.astype(float_type), inner_size, outer_size)
    back_long, taps_grad = correlate(
        up_real,
        up_imag,
        input_real,
        input_imag,
        taps_real,
        taps_imag,
        inner_size,
        outer_size,
        taps_factor,
    )
    grad_mixed = lax.all_to_all(back_long, "seq", split_axis=1, concat_axis=0, tiled=True)
    conv_float = conv_out.astype(float_type)
    grad_float = grad_mixed.astype(float_type)
    mixed_out = (query_proj.astype(float_type) * conv_float).astype(half_type)
    grad_key = (grad_float * value_proj.astype(float_type)).astype(half_type)
    grad_value = (grad_float * key_proj.astype(float_type)).astype(half_type)
    selector = (jnp.arange(filter_taps.shape[0], dtype=jnp.int32) == local_group).astype(float_type)
    filter_grad = lax.psum_scatter(
        selector[:, None] * taps_grad, "seq", scatter_dimension=1, tiled=True
    )
    weight_grad = weight_sum(layer_input, grad_query, weight_factor)
    return (mixed_out, grad_query, grad_key, grad_value, filter_grad, weight_grad)


def solution(mesh):
    placed = (
        P("chan", "seq"),
        P("chan", "seq"),
        P("chan", "seq"),
        P("chan", "seq"),
        P("chan", "seq"),
        P("chan", "seq"),
    )
    return jax.shard_map(
        per_device,
        mesh=mesh,
        in_specs=placed,
        out_specs=(
            P("chan", "seq"),
            P("chan", "seq"),
            P("chan", "seq"),
            P("chan", "seq"),
            P("chan", "seq"),
            P("seq", "chan"),
        ),
        check_vma=False,
    )
```

profile of v0, /device:TPU:0, one launch (start us, length us, event | category | flops | bytes accessed | tf_op | source)
XLA Modules:
  0.0 755.0 jit_solution(1742604908414005586)
XLA Ops:
  10.8 10.7 %all-to-all-start.2 = ((bf16[32,32,512]{2,1,0:T(8,128)(2,1)}), bf16[32,32,512]{2,1,0:T(8,128)(2,1)S(1)}, u32[]{:S(2)}, u32[]{:S(2)}) async-start(bf16[32,32,512]{2,1,0:T(8,128)(2,1)} %bitcast.24), calls=%async_computation.2 | async-start | bytes 2097152 | tf_op jit(solution)/shard_map/all_to_all | solution.py:136
  25.0 95.5 %all_gather.6 = f32[2,16384]{1,0:T(2,128)S(1)} all-gather(f32[2,512]{1,0:T(2,128)S(1)} %copy-done.13), channel_id=1, replica_groups=mesh['seq'=32,'chan'=4] {'seq'}, dimensions={1}, use_global_device_ids=true | all-gather | bytes 135168 | tf_op jit(solution)/shard_map/all_gather | solution.py:127
  131.4 7.3 fusion.56
  138.7 7.3 fusion.58
  145.9 7.4 convolution_add_fusion.1
  153.4 7.3 convolution_subtract_fusion.1
  160.7 5.3 fusion.47
  171.0 4.9 convolution_subtract_fusion
  175.9 5.1 convolution_add_fusion
  190.3 18.0 %all_to_all.52 = bf16[32,32,512]{2,0,1:T(8,128)(2,1)S(1)} all-to-all(bf16[32,32,512]{2,0,1:T(8,128)(2,1)S(1)} %copy.120), channel_id=1, replica_groups=mesh['seq'=32,'chan'=4] {'seq'}, dimensions={1} | all-to-all | bytes 2097152 | tf_op jit(solution)/shard_map/all_to_all | solution.py:149
  211.1 8.6 %all-to-all-start = ((bf16[32,32,512]{2,1,0:T(8,128)(2,1)}), bf16[32,32,512]{2,1,0:T(8,128)(2,1)S(1)}, u32[]{:S(2)}, u32[]{:S(2)}) async-start(bf16[32,32,512]{2,1,0:T(8,128)(2,1)} %bitcast.9), calls=%async_computation | async-start | bytes 2097152 | tf_op jit(solution)/shard_map/all_to_all | solution.py:131
  220.5 13.4 %all-to-all-done = bf16[32,32,512]{2,1,0:T(8,128)(2,1)S(1)} async-done(((bf16[32,32,512]{2,1,0:T(8,128)(2,1)}), bf16[32,32,512]{2,1,0:T(8,128)(2,1)S(1)}, u32[]{:S(2)}, u32[]{:S(2)}) %all-to-all-start) | async-done | bytes 1048608 | tf_op jit(solution)/shard_map/all_to_all | solution.py:131
  238.9 9.2 %fusion.50 = f32[32,256,128]{2,1,0:T(8,128)} fusion(f32[32,128,256]{2,1,0:T(8,128)S(1)} %fusion.80, f32[32,128,256]{2,1,0:T(8,128)S(1)} %fusion.84, f32[256,128]{0,1:T(8,128)S(1)} %copy.96, f32[256,128]{0,1:T(8,128)S(1)} %copy.94), kind=kOutput, calls=%fused_computation.71 | convolution fusion | flops 1614004224 | bytes 12845056 | tf_op jit(solution)/shard_map/pkt,tj->pkj/dot_general | solution.py:34
  248.1 7.1 fusion.52
  255.2 7.9 %convolution_subtract_fusion.3 = f32[32,256,128]{2,1,0:T(8,128)S(1)} fusion(f32[32,256,128]{2,1,0:T(8,128)S(1)} %fusion.52, f32[32,128,256]{2,1,0:T(8,128)S(1)} %fusion.80, f32[32,128,256]{2,1,0:T(8,128)S(1)} %fusion.84, f32[256,128]{0,1:T(8,128)S(1)} %copy.96, f32[256,128]{0,1:T(8,128)S(1)} %copy.94), kind=kOutput, calls=%fused_computation.48 | convolution fusion | flops 1615052800 | bytes 17039360 | tf_op jit(solution)/shard_map/pkt,tj->pkj/dot_general | solution.py:34
  263.1 11.4 %subtract_reduce_fusion = (f32[256,128]{1,0:T(8,128)S(1)}, f32[256,128]{1,0:T(8,128)}, f32[32,256,128]{2,1,0:T(8,128)S(1)}) fusion(f32[32,256,128]{2,1,0:T(8,128)S(1)} %copy-done.3, f32[32,256,128]{2,1,0:T(8,128)S(1)} %copy-done.1, f32[32,256,128]{2,1,0:T(8,128)S(1)} %convolution_subtract_fusion.3, f32[32,256,128]{2,1,0:T(8,128)} %fusion.50, ...), kind=kOutput, calls=%fused_computation.13 | convolution fusion | flops 1623359488 | bytes 29884416 | tf_op jit(solution)/shard_map/pkt,tj->pkj/dot_general | solution.py:34
  274.6 4.9 fusion.45
  284.4 5.4 convolution_subtract_fusion.2
  289.8 4.9 convolution_add_fusion.2
  313.4 5.0 copy.143
  318.5 5.0 all-to-all-done.1
  325.3 12.8 %convolution_bitcast_fusion = f32[4096,1024]{0,1:T(8,128)} fusion(bf16[1024,512]{1,0:T(8,128)(2,1)} %get-tuple-element.35, bf16[4096,512]{1,0:T(8,128)(2,1)} %all-gather.2.cloned.1.call-done), kind=kOutput, calls=%fused_computation | convolution fusion | flops 4294967296 | bytes 22020096 | tf_op jit(solution)/shard_map/it,jt->ij/dot_general | solution.py:106
  338.1 185.3 %reduce-scatter.7.cloned.1.call-done = f32[512,2]{1,0:T(8,128)} async-done(((f32[16384,2]{1,0:T(8,128)}), f32[512,2]{1,0:T(8,128)}) %reduce-scatter.7.cloned.1.call-update) | async-done | bytes 4112
  525.1 220.3 %reduce-scatter.5.cloned.1.call-done = f32[128,1024]{0,1:T(8,128)} async-done(((f32[4096,1024]{0,1:T(8,128)}), f32[128,1024]{0,1:T(8,128)}) %reduce-scatter.5.cloned.1.call-update) | async-done | bytes 524304 | tf_op jit(solution)/shard_map/reduce_scatter | solution.py:105
  (87 shorter events, 68.6 us)
Async XLA Ops:
  8.0 17.0 %copy-start.13 = (f32[2,512]{1,0:T(2,128)S(1)}, f32[2,512]{1,0:T(2,128)}, u32[]{:S(2)}) copy-start(f32[2,512]{1,0:T(2,128)} %param.10) | copy-start | bytes 12292
  10.8 115.1 %all-to-all-start.2 = ((bf16[32,32,512]{2,1,0:T(8,128)(2,1)}), bf16[32,32,512]{2,1,0:T(8,128)(2,1)S(1)}, u32[]{:S(2)}, u32[]{:S(2)}) async-start(bf16[32,32,512]{2,1,0:T(8,128)(2,1)} %bitcast.24), calls=%async_computation.2 | async-start | bytes 2097152 | tf_op jit(solution)/shard_map/all_to_all | solution.py:136
  23.5 211.7 %copy-start.7 = (f32[256,256]{1,0:T(8,128)}, f32[256,256]{1,0:T(8,128)S(1)}, u32[]{:S(2)}) copy-start(f32[256,256]{1,0:T(8,128)S(1)} %fusion.104) | copy-start | bytes 786436
  153.4 22.5 %copy-start = (f32[32,256,128]{2,1,0:T(8,128)}, f32[32,256,128]{2,1,0:T(8,128)S(1)}, u32[]{:S(2)}) copy-start(f32[32,256,128]{2,1,0:T(8,128)S(1)} %convolution_add_fusion.1) | copy-start | bytes 12582916
  160.7 15.2 %copy-start.2 = (f32[32,256,128]{2,1,0:T(8,128)}, f32[32,256,128]{2,1,0:T(8,128)S(1)}, u32[]{:S(2)}) copy-start(f32[32,256,128]{2,1,0:T(8,128)S(1)} %convolution_subtract_fusion.1) | copy-start | bytes 12582916
  189.7 18.6 %copy-start.10 = (bf16[1024,512]{1,0:T(8,128)(2,1)S(1)}, bf16[1024,512]{1,0:T(8,128)(2,1)}, u32[]{:S(2)}) copy-start(bf16[1024,512]{1,0:T(8,128)(2,1)} %param.8) | copy-start | bytes 3145732
  189.7 18.6 %copy-start.11 = (bf16[1024,512]{1,0:T(8,128)(2,1)S(1)}, bf16[1024,512]{1,0:T(8,128)(2,1)}, u32[]{:S(2)}) copy-start(bf16[1024,512]{1,0:T(8,128)(2,1)} %param.9) | copy-start | bytes 3145732
  211.1 22.8 %all-to-all-start = ((bf16[32,32,512]{2,1,0:T(8,128)(2,1)}), bf16[32,32,512]{2,1,0:T(8,128)(2,1)S(1)}, u32[]{:S(2)}, u32[]{:S(2)}) async-start(bf16[32,32,512]{2,1,0:T(8,128)(2,1)} %bitcast.9), calls=%async_computation | async-start | bytes 2097152 | tf_op jit(solution)/shard_map/all_to_all | solution.py:131
  219.7 105.6 %all-gather.2.cloned.1.call-start = ((), (), s32[]{:S(2)}) async-start(), calls=%async_computation.6 | async-start | bytes 5242880 | tf_op jit(solution)/shard_map/all_gather | solution.py:104
  238.9 16.3 %copy-start.4 = (f32[32,128,256]{2,1,0:T(8,128)}, f32[32,128,256]{2,1,0:T(8,128)S(1)}, u32[]{:S(2)}) copy-start(f32[32,128,256]{2,1,0:T(8,128)S(1)} %fusion.80) | copy-start | bytes 12582916
  255.2 7.9 %copy-start.1 = (f32[32,256,128]{2,1,0:T(8,128)S(1)}, f32[32,256,128]{2,1,0:T(8,128)}, u32[]{:S(2)}) copy-start(f32[32,256,128]{2,1,0:T(8,128)} %copy-done) | copy-start | bytes 12582916
  255.2 7.9 %copy-start.3 = (f32[32,256,128]{2,1,0:T(8,128)S(1)}, f32[32,256,128]{2,1,0:T(8,128)}, u32[]{:S(2)}) copy-start(f32[32,256,128]{2,1,0:T(8,128)} %copy-done.2) | copy-start | bytes 12582916
  294.7 3.7 copy-start.8
  302.9 6.4 copy-start.12
  302.9 8.4 %copy-start.9 = (f32[256,256]{1,0:T(8,128)S(1)}, f32[256,256]{1,0:T(8,128)}, u32[]{:S(2)}) copy-start(f32[256,256]{1,0:T(8,128)} %copy-done.7) | copy-start | bytes 786436
  305.2 18.3 %all-to-all-start.1 = ((bf16[32,32,512]{2,0,1:T(8,128)(2,1)}), bf16[32,32,512]{2,0,1:T(8,128)(2,1)S(1)}, u32[]{:S(2)}, u32[]{:S(2)}) async-start(bf16[32,32,512]{2,0,1:T(8,128)(2,1)} %copy.107), calls=%async_computation.1 | async-start | bytes 2097152 | tf_op jit(solution)/shard_map/all_to_all | solution.py:134
  309.2 214.2 %reduce-scatter.7.cloned.1.call-start = ((), (), s32[]{:S(2)}) async-start(), calls=%async_computation.8 | async-start | bytes 8650752
  318.4 5.1 copy-start.5
  318.4 5.1 copy-start.6
  318.4 426.9 %reduce-scatter.5.cloned.1.call-start = ((), (), s32[]{:S(2)}) async-start(), calls=%async_computation.7 | async-start | bytes 17301504 | tf_op jit(solution)/shard_map/reduce_scatter | solution.py:105
Sparse Core Ops, SparseCore 0:
  222.2 47.6 all-gather.1
Sparse Core Ops, SparseCore 1:
  318.5 204.9 reduce-scatter.6
  525.7 219.6 reduce-scatter.4
where the time goes:
time: 763 us; the launch traced here: 755 us
  waiting for transfers between devices  425 us (56%)
  matrix products  149 us (20%)
  blocking collectives  114 us (15%)
  starting transfers between devices  23.5 us (3%)
  between operations  16.3 us (2%)
  local copies, waits for them, and re-layouts  15.9 us (2%)
  other arithmetic  12 us (2%)
    reduce_scatter x1, waiting for transfers between devices, weight_sum(): lax.psum_scatter(jnp.einsum('it,jt->ij', gathered, grad_query, preferred_...  220 us
    unnamed x4, waiting for transfers between devices  186 us
    dot_general x36, matrix products, contract(): jnp.einsum(pattern, first_op, second_op, precision=lax.Precision.HIGHEST,...  136 us
    all_gather x1, blocking collectives, per_device(): full_taps = lax.all_gather(filter_taps, 'seq', axis=1, tiled=True)  95.5 us
    all_to_all x1, blocking collectives, per_device(): lax.all_to_all(back_long, 'seq', split_axis=1, concat_axis=0, tiled=True)  18 us
  transfers between devices with their start and end apart: 6, of which 4 were waited for; matrix products, arithmetic and copies ran while one was open for 14% of the time, Pallas kernels for 0%

commit v1 on v0

v1 whole, which is shorter than its diff:
```python
import functools
import math

import jax
import jax.numpy as jnp
from jax import lax
from jax.experimental import pallas as pl
from jax.experimental.pallas import tpu as pltpu
from jax.sharding import PartitionSpec as P

GROUP = 512
F32 = jnp.float32
BF16 = jnp.bfloat16
MESH = pl.DeviceIdType.MESH

N = 32
CH = 32
T = 512
B = 256
NB = N * T // B
PAD = 8
ROWS = N * CH
KINDS = 6
MIXED, UP, TAPS, CONV, BACK, FILT = range(KINDS)


def seq_copy(src, dst, kind, peer, sems, me):
    send, recv = sems
    return pltpu.make_async_remote_copy(
        src_ref=src,
        dst_ref=dst,
        send_sem=send.at[kind, peer],
        recv_sem=recv.at[kind, me],
        device_id={"seq": peer},
        device_id_type=MESH,
    )


def for_peers(me, body):
    def step(i, carry):
        body(lax.rem(me + i, N))
        return carry

    lax.fori_loop(1, N, step, 0)


def loop(n, body, start=0):
    def step(i, carry):
        body(i)
        return carry

    lax.fori_loop(start, n, step, 0)


def kernel(
    x_ref,
    q_ref,
    k_ref,
    v_ref,
    taps_ref,
    g_ref,
    mixed_out_ref,
    grad_query_ref,
    grad_key_ref,
    grad_value_ref,
    filter_grad_ref,
    weight_grad_ref,
    mixed_send,
    up_send,
    taps_send,
    taps_all,
    mixed_all,
    up_all,
    mixed_flip,
    toeplitz,
    acc,
    conv_send,
    back_send,
    conv_all,
    back_all,
    filt_part,
    filt_send,
    filt_all,
    x_all,
    part_a,
    part_b,
    first_in,
    first_out,
    second_in,
    second_out,
    third_in,
    send_sem,
    recv_sem,
    x_send_sem,
    x_recv_sem,
    r_send_sem,
    r_recv_sem,
    z_send_sem,
    z_recv_sem,
):
    me = lax.axis_index("seq")
    chan = lax.axis_index("chan")
    ix = me // 8
    iz = lax.rem(me // 4, 2)
    iy = lax.rem(me, 4)
    sems = (send_sem, recv_sem)

    barrier = pltpu.get_barrier_semaphore()
    for_peers(
        me,
        lambda peer: pl.semaphore_signal(
            barrier, inc=1, device_id={"seq": peer}, device_id_type=MESH
        ),
    )
    core_peer = chan + 1 - 2 * lax.rem(chan, 2)
    near_peer = lax.rem(chan + 2, 4)
    for peer in (core_peer, near_peer):
        pl.semaphore_signal(barrier, inc=1, device_id={"chan": peer}, device_id_type=MESH)

    def make_mixed(r):
        rows = pl.ds(pl.multiple_of(r * 128, 128), 128)
        prod = (k_ref[rows, :].astype(F32) * v_ref[rows, :].astype(F32)).astype(BF16)
        mixed_send[0, rows, :] = prod[:, :B]
        mixed_send[1, rows, :] = prod[:, B:]

    def make_up(r):
        rows = pl.ds(pl.multiple_of(r * 128, 128), 128)
        prod = (g_ref[rows, :].astype(F32) * q_ref[rows, :].astype(F32)).astype(BF16)
        up_send[0, rows, :] = prod[:, :B]
        up_send[1, rows, :] = prod[:, B:]

    for g in range(2):
        for c in range(4):
            taps_send[g, c : c + 1, :] = taps_ref[g : g + 1, c * 128 : (c + 1) * 128]
        taps_send[g, 4:8, :] = jnp.zeros((4, 128), F32)
    loop(ROWS // 128, make_mixed)
    pl.semaphore_wait(barrier, N + 1)

    def chan_rows(peer):
        return pl.ds(pl.multiple_of(peer * CH, CH), CH)

    def taps_copy(peer):
        return seq_copy(taps_send.at[peer // 16], taps_all.at[me], TAPS, peer, sems, me)

    def mixed_copy(peer):
        return seq_copy(
            mixed_send.at[:, chan_rows(peer), :],
            mixed_all.at[pl.ds(PAD + 2 * me, 2)],
            MIXED,
            peer,
            sems,
            me,
        )

    def up_copy(peer):
        return seq_copy(
            up_send.at[:, chan_rows(peer), :],
            up_all.at[pl.ds(2 * me, 2)],
            UP,
            peer,
            sems,
            me,
        )

    def conv_copy(peer):
        return seq_copy(
            conv_send.at[pl.ds(2 * peer, 2)],
            conv_all.at[:, chan_rows(me), :],
            CONV,
            peer,
            sems,
            me,
        )

    def back_copy(peer):
        return seq_copy(
            back_send.at[pl.ds(2 * peer, 2)],
            back_all.at[:, chan_rows(me), :],
            BACK,
            peer,
            sems,
            me,
        )

    def filt_copy(peer):
        return seq_copy(filt_send.at[peer], filt_all.at[me], FILT, peer, sems, me)

    def wait_all(kind, dst_of, src_any):
        def one(peer):
            pltpu.make_async_remote_copy(
                src_ref=src_any,
                dst_ref=dst_of(peer),
                send_sem=send_sem.at[kind, peer],
                recv_sem=recv_sem.at[kind, peer],
                device_id={"seq": peer},
                device_id_type=MESH,
            ).wait_recv()

        for_peers(me, one)

    for_peers(me, lambda peer: taps_copy(peer).start())
    for_peers(me, lambda peer: mixed_copy(peer).start())
    loop(ROWS // 128, make_up)
    for_peers(me, lambda peer: up_copy(peer).start())

    taps_all[me] = taps_send[me // 16]
    mixed_all[pl.ds(PAD + 2 * me, 2)] = mixed_send[:, chan_rows(me), :]
    up_all[pl.ds(2 * me, 2)] = up_send[:, chan_rows(me), :]
    mixed_all[:PAD] = jnp.zeros((PAD, CH, B), BF16)
    up_all[NB:] = jnp.zeros((PAD, CH, B), BF16)

    wait_all(TAPS, lambda peer: taps_all.at[peer], taps_send.at[0])
    row_id = lax.broadcasted_iota(jnp.int32, (B, B), 0)
    col_id = lax.broadcasted_iota(jnp.int32, (B, B), 1)

    def sheared(src, half):
        piece = taps_all[src]
        wide = jnp.concatenate(
            [piece[2 * half : 2 * half + 1, :], piece[2 * half + 1 : 2 * half + 2, :]], axis=1
        )
        return pltpu.roll(jnp.broadcast_to(wide, (B, B)), 0, 1, stride=1, stride_axis=0)

    acc[...] = jnp.zeros((B, B), F32)

    def make_tiles(s):
        for half in range(2):
            now = sheared(s, half)
            toeplitz[2 * s + half] = jnp.where(col_id >= row_id, now, acc[...]).astype(BF16)
            acc[...] = now

    loop(N, make_tiles)

    wait_all(MIXED, lambda peer: mixed_all.at[pl.ds(PAD + 2 * peer, 2)], mixed_send.at[:, :CH, :])

    def hand_back(i, copy, send, dest):
        for r in range(4):
            peer = 4 * i + r

            @pl.when(peer != me)
            def _():
                copy(peer).start()

            @pl.when(peer == me)
            def _():
                dest[:, chan_rows(me), :] = send[pl.ds(2 * me, 2)]

    def conv_chunk(step):
        i = lax.rem(me // 4 + step, 8)
        acc[...] = jnp.zeros((B, B), F32)

        def some(j):
            part = None
            for u in range(8):
                m = 8 * j + u
                lhs = mixed_all[pl.ds(PAD + 8 * i - m, 8)].reshape(B, B)
                term = jnp.dot(lhs, toeplitz[m], preferred_element_type=F32)
                part = term if part is None else part + term
            acc[...] += part

        loop(i + 1, some)
        conv_send[pl.ds(8 * i, 8)] = acc[...].astype(BF16).reshape(8, CH, B)
        hand_back(i, conv_copy, conv_send, conv_all)

    own_x = pl.ds(pl.multiple_of(chan * ROWS, ROWS), ROWS)
    near_x = pl.ds(pl.multiple_of(near_peer * ROWS, ROWS), ROWS)

    def x_copy(slot, src, rows, peer):
        return pltpu.make_async_remote_copy(
            src_ref=src,
            dst_ref=x_all.at[rows, :],
            send_sem=x_send_sem.at[slot],
            recv_sem=x_recv_sem.at[slot],
            device_id={"chan": peer},
            device_id_type=MESH,
        )

    x_core = x_copy(0, x_ref, own_x, core_peer)
    x_near = x_copy(1, x_ref, own_x, near_peer)
    x_pass = x_copy(2, x_all.at[near_x, :], near_x, core_peer)
    x_core.start()
    x_near.start()
    x_all[own_x, :] = x_ref[...]
    loop(8, conv_chunk)

    wait_all(UP, lambda peer: up_all.at[pl.ds(2 * peer, 2)], up_send.at[:, :CH, :])

    def back_chunk(step):
        i = lax.rem(me // 4 + step, 8)
        acc[...] = jnp.zeros((B, B), F32)

        def some(j):
            part = None
            for u in range(8):
                m = 8 * j + u
                lhs = up_all[pl.ds(8 * i + m, 8)].reshape(B, B)
                term = lax.dot_general(
                    lhs, toeplitz[m], (((1,), (1,)), ((), ())), preferred_element_type=F32
                )
                part = term if part is None else part + term
            acc[...] += part

        loop(8 - i, some)
        back_send[pl.ds(8 * i, 8)] = acc[...].astype(BF16).reshape(8, CH, B)
        hand_back(i, back_copy, back_send, back_all)

    loop(8, back_chunk)
    x_near.wait_recv()
    x_pass.start()

    wait_all(CONV, lambda peer: conv_all.at[:, chan_rows(peer), :], conv_send.at[:2])

    def use_conv(r):
        rows = pl.ds(pl.multiple_of(r * 128, 128), 128)
        for half in range(2):
            cols = slice(half * B, (half + 1) * B)
            conv = conv_all[half, rows, :].astype(F32)
            grad_query_ref[rows, cols] = (g_ref[rows, cols].astype(F32) * conv).astype(BF16)
            mixed_out_ref[rows, cols] = (q_ref[rows, cols].astype(F32) * conv).astype(BF16)

    loop(ROWS // 128, use_conv)
    x_core.wait_recv()
    x_pass.wait_recv()

    def weight_share(r):
        px, pz = r // 2, lax.rem(r, 2)
        rows = pl.ds(pl.multiple_of(r * 512, 512), 512)
        for half in range(2):
            share = lax.dot_general(
                x_all[rows, :],
                grad_query_ref[half * 512 : (half + 1) * 512, :],
                (((1,), (1,)), ((), ())),
                preferred_element_type=F32,
            ).astype(BF16)
            if half == 0:
                part_a[px, pz] = share.reshape(4, 128, 512)
            else:
                for py in range(4):
                    part_b[py, pz, px] = share[py * 128 : (py + 1) * 128, :]

    loop(8, weight_share)

    def x_peer(d):
        return lax.rem(ix + d, 4) * 8 + iz * 4 + iy

    def y_peer(d):
        return ix * 8 + iz * 4 + lax.rem(iy + d, 4)

    def ring_copy(half, stage, slot, src, dst, peer):
        return pltpu.make_async_remote_copy(
            src_ref=src,
            dst_ref=dst,
            send_sem=r_send_sem.at[half, stage, slot],
            recv_sem=r_recv_sem.at[half, stage, slot],
            device_id={"seq": peer},
            device_id_type=MESH,
        )

    def ring_copies(half, stage, part, inbox, index, peer_of):
        up, down, far = (lax.rem(index + d, 4) for d in (1, 3, 2))
        return (
            ring_copy(half, stage, 0, part.at[far, 0], inbox.at[0], peer_of(1)),
            ring_copy(half, stage, 1, part.at[far, 1], inbox.at[1], peer_of(3)),
            ring_copy(half, stage, 2, part.at[up, 1], inbox.at[2], peer_of(1)),
            ring_copy(half, stage, 3, part.at[down, 0], inbox.at[3], peer_of(3)),
            ring_copy(half, stage, 4, part.at[up, 0], inbox.at[4], peer_of(1)),
            ring_copy(half, stage, 5, part.at[down, 1], inbox.at[5], peer_of(3)),
        )

    def ring_start(copies):
        for c in copies[:4]:
            c.start()

    def ring_middle(copies, part, inbox, index, blocks):
        for slot, there, side in ((0, 1, 0), (1, 3, 1)):
            copies[slot].wait_recv()
            target = lax.rem(index + there, 4)

            def add(e):
                total = part[target, side, e].astype(F32) + inbox[slot, e].astype(F32)
                part[target, side, e] = total.astype(BF16)

            loop(blocks, add)
            copies[4 + slot].start()

    def ring_end(copies, part, inbox, index, blocks, store):
        for slot in (2, 3, 4, 5):
            copies[slot].wait_recv()

        def add(e):
            for side, one, two in ((0, 4, 3), (1, 5, 2)):
                total = part[index, side, e].astype(F32) + (
                    inbox[one, e].astype(F32) + inbox[two, e].astype(F32)
                )
                store(side, e, total)

        loop(blocks, add)

    halves = (
        (part_a, ix, x_peer, iy, y_peer),
        (part_b, iy, y_peer, ix, x_peer),
    )
    firsts = []
    for half, (part, index, peer_of, _, _) in enumerate(halves):
        copies = ring_copies(half, 0, part, first_in.at[half], index, peer_of)
        ring_start(copies)
        firsts.append(copies)

    flip = (row_id + col_id == B - 1).astype(BF16)
    for c in range(8):
        piece = mixed_all[PAD + 8 * c : PAD + 8 * c + 8].reshape(B, B)
        mixed_flip[:, c * B : (c + 1) * B] = lax.dot_general(
            flip, piece, (((1,), (1,)), ((), ())), preferred_element_type=F32
        ).astype(BF16)

    def filter_tile(i, m):
        depth = (8 - i) * B
        corr = jnp.dot(
            mixed_flip[:, :depth],
            up_all[pl.ds(m, 8 * (8 - i))].reshape(depth, B),
            preferred_element_type=F32,
        )
        turned = pltpu.roll(corr, 1, 1, stride=1, stride_axis=0)
        above = jnp.where(col_id <= row_id, turned, 0.0)
        below = turned - above
        filt_part[0, m] = jnp.sum(above.reshape(B // 8, 8, B), axis=0)
        filt_part[1, m] = jnp.sum(below.reshape(B // 8, 8, B), axis=0)

    def filter_some(i):
        loop(8, lambda u: filter_tile(i, 8 * i + u))

    for i in range(4):
        filter_some(i)
    for half, (part, index, _, _, _) in enumerate(halves):
        ring_middle(firsts[half], part, first_in.at[half], index, 4)
    for i in range(4, 8):
        filter_some(i)

    filt_part[1, NB] = jnp.zeros((8, B), F32)
    taps_factor = 1.0 / math.sqrt(GROUP * N * T)

    def filter_rows(s):
        for half in range(2):
            m = 2 * s + half
            both = jnp.sum(filt_part[0, m] + filt_part[1, m + 1], axis=0, keepdims=True)
            filt_send[s, 2 * half : 2 * half + 1, :] = both[:, :128] * taps_factor
            filt_send[s, 2 * half + 1 : 2 * half + 2, :] = both[:, 128:] * taps_factor
        filt_send[s, 4:8, :] = jnp.zeros((4, 128), F32)

    loop(N, filter_rows)
    for_peers(me, lambda peer: filt_copy(peer).start())
    filt_all[me] = filt_send[me]

    wait_all(BACK, lambda peer: back_all.at[:, chan_rows(peer), :], back_send.at[:2])

    def use_back(r):
        rows = pl.ds(pl.multiple_of(r * 128, 128), 128)
        for half in range(2):
            cols = slice(half * B, (half + 1) * B)
            back = back_all[half, rows, :].astype(F32)
            grad_key_ref[rows, cols] = (v_ref[rows, cols].astype(F32) * back).astype(BF16)
            grad_value_ref[rows, cols] = (k_ref[rows, cols].astype(F32) * back).astype(BF16)

    loop(ROWS // 128, use_back)

    seconds = []
    for half, (part, index, _, across, across_peer) in enumerate(halves):

        def store(side, e, total):
            first_out[half, e, side, 0] = total.astype(BF16)

        ring_end(firsts[half], part, first_in.at[half], index, 4, store)
        copies = ring_copies(
            half, 1, first_out.at[half], second_in.at[half], across, across_peer
        )
        ring_start(copies)
        seconds.append(copies)
    for half, (_, _, _, across, _) in enumerate(halves):
        ring_middle(seconds[half], first_out.at[half], second_in.at[half], across, 1)

    wait_all(FILT, lambda peer: filt_all.at[peer], filt_send.at[0])
    for g in range(2):
        total = jnp.sum(filt_all[16 * g : 16 * g + 16], axis=0)
        for c in range(4):
            filter_grad_ref[g : g + 1, c * 128 : (c + 1) * 128] = total[c : c + 1, :]

    thirds = []
    other = ix * 8 + (1 - iz) * 4 + iy
    for half, (_, _, _, across, _) in enumerate(halves):

        def keep(side, e, total):
            second_out[half, side] = total.astype(BF16)

        ring_end(seconds[half], first_out.at[half], second_in.at[half], across, 1, keep)
        copy = pltpu.make_async_remote_copy(
            src_ref=second_out.at[half, 1 - iz],
            dst_ref=third_in.at[half],
            send_sem=z_send_sem.at[half],
            recv_sem=z_recv_sem.at[half],
            device_id={"seq": other},
            device_id_type=MESH,
        )
        copy.start()
        thirds.append(copy)
    weight_factor = 1.0 / math.sqrt(N * T)
    for half in range(2):
        thirds[half].wait_recv()
        total = second_out[half, iz].astype(F32) + third_in[half].astype(F32)
        weight_grad_ref[:, half * 512 : (half + 1) * 512] = total * weight_factor

    for make in (taps_copy, mixed_copy, up_copy, conv_copy, back_copy, filt_copy):
        for_peers(me, lambda peer: make(peer).wait_send())
    for c in (x_core, x_near, x_pass, *firsts[0], *firsts[1], *seconds[0], *seconds[1], *thirds):
        c.wait_send()


def per_device(layer_input, query_proj, key_proj, value_proj, filter_taps, grad_out):
    vmem = pl.BlockSpec(memory_space=pltpu.VMEM)
    rows = jax.ShapeDtypeStruct((ROWS, T), BF16)
    return tuple(
        pl.pallas_call(
            kernel,
            out_shape=(
                rows,
                rows,
                rows,
                rows,
                jax.ShapeDtypeStruct((2, T), F32),
                jax.ShapeDtypeStruct((128, ROWS), F32),
            ),
            in_specs=[vmem] * 6,
            out_specs=[vmem] * 6,
            scratch_shapes=[
                pltpu.VMEM((2, ROWS, B), BF16),
                pltpu.VMEM((2, ROWS, B), BF16),
                pltpu.VMEM((2, 8, 128), F32),
                pltpu.VMEM((N, 8, 128), F32),
                pltpu.VMEM((PAD + NB, CH, B), BF16),
                pltpu.VMEM((NB + PAD, CH, B), BF16),
                pltpu.VMEM((B, NB * CH), BF16),
                pltpu.VMEM((NB, B, B), BF16),
                pltpu.VMEM((B, B), F32),
                pltpu.VMEM((NB, CH, B), BF16),
                pltpu.VMEM((NB, CH, B), BF16),
                pltpu.VMEM((2, ROWS, B), BF16),
                pltpu.VMEM((2, ROWS, B), BF16),
                pltpu.VMEM((2, NB + 1, 8, B), F32),
                pltpu.VMEM((N, 8, 128), F32),
                pltpu.VMEM((N, 8, 128), F32),
                pltpu.VMEM((4 * ROWS, T), BF16),
                pltpu.VMEM((4, 2, 4, 128, 512), BF16),
                pltpu.VMEM((4, 2, 4, 128, 512), BF16),
                pltpu.VMEM((2, 6, 4, 128, 512), BF16),
                pltpu.VMEM((2, 4, 2, 1, 128, 512), BF16),
                pltpu.VMEM((2, 6, 1, 128, 512), BF16),
                pltpu.VMEM((2, 2, 128, 512), BF16),
                pltpu.VMEM((2, 128, 512), BF16),
                pltpu.SemaphoreType.DMA((KINDS, N)),
                pltpu.SemaphoreType.DMA((KINDS, N)),
                pltpu.SemaphoreType.DMA((3,)),
                pltpu.SemaphoreType.DMA((3,)),
                pltpu.SemaphoreType.DMA((2, 2, 6)),
                pltpu.SemaphoreType.DMA((2, 2, 6)),
                pltpu.SemaphoreType.DMA((2,)),
                pltpu.SemaphoreType.DMA((2,)),
            ],
            compiler_params=pltpu.CompilerParams(
                collective_id=0, has_side_effects=True, vmem_limit_bytes=60 * 2**20
            ),
        )(layer_input, query_proj, key_proj, value_proj, filter_taps, grad_out)
    )


def solution(mesh):
    placed = (P("chan", "seq"),) * 6
    return jax.shard_map(
        per_device,
        mesh=mesh,
        in_specs=placed,
        out_specs=(P("chan", "seq"),) * 5 + (P("seq", "chan"),),
        check_vma=False,
    )
```

time: 763 us -> 163 us (0.21); the launches traced: 755 us -> 163 us
  waiting for transfers between devices: 425 us -> 0 us
  Pallas kernels: 0 us -> 154 us
  matrix products: 149 us -> 0 us
  blocking collectives: 114 us -> 0 us
  starting transfers between devices: 23.5 us -> 0 us
  between operations: 16.3 us -> 0.66 us
  other arithmetic: 12 us -> 0 us
  local copies, waits for them, and re-layouts: 15.9 us -> 7.92 us
    reduce_scatter x1 -> x0, waiting for transfers between devices: 220 us -> none  [weight_sum(): lax.psum_scatter(jnp.einsum('it,jt->ij', gathered, grad_query, preferred_...]
    unnamed x4 -> x0, waiting for transfers between devices: 186 us -> none
    pallas_call x0 -> x1, Pallas kernels: none -> 154 us  [per_device(): pl.pallas_call(kernel, out_shape=(rows, rows, rows, rows, jax.ShapeDtypeS...]
    dot_general x37 -> x0, matrix products: 149 us -> none  [the longest x36 136 us: contract(): jnp.einsum(pattern, first_op, second_op, precision=lax.Precision.HIGHEST,...]
    all_gather x1 -> x0, blocking collectives: 95.5 us -> none  [per_device(): full_taps = lax.all_gather(filter_taps, 'seq', axis=1, tiled=True)]
    all_to_all x3 -> x0, starting transfers between devices: 23.4 us -> none  [the longest x1 10.7 us: per_device(): lax.all_to_all(upstream, 'seq', split_axis=0, concat_axis=1, tiled=True)]
    all_to_all x3 -> x0, waiting for transfers between devices: 18.4 us -> none  [the longest x1 13.4 us: per_device(): lax.all_to_all(mixed_in, 'seq', split_axis=0, concat_axis=1, tiled=True)]
    all_to_all x1 -> x0, blocking collectives: 18 us -> none  [per_device(): lax.all_to_all(back_long, 'seq', split_axis=1, concat_axis=0, tiled=True)]
  transfers between devices with their start and end apart: 6 -> 0, of which waited for: 4 -> 0; matrix products, arithmetic and copies ran while one was open for 14% -> 0% of each run, Pallas kernels for 0% -> 0%
where the time goes in v1:
time: 163 us
  Pallas kernels  154 us (94%)
  local copies, waits for them, and re-layouts  7.92 us (5%)
    pallas_call x1, Pallas kernels, per_device(): pl.pallas_call(kernel, out_shape=(rows, rows, rows, rows, jax.ShapeDtypeS...  154 us
    unnamed x16, local copies, waits for them, and re-layouts  7.92 us

profile of v1, /device:TPU:0, one launch (start us, length us, event | category | flops | bytes accessed | tf_op | source)
XLA Modules:
  0.0 163.1 jit_solution(14312428739400963737)
XLA Ops:
  0.6 154.5 %shard_map.109 = (bf16[1024,512]{1,0:T(8,128)(2,1)}, bf16[1024,512]{1,0:T(8,128)(2,1)}, bf16[1024,512]{1,0:T(8,128)(2,1)}, bf16[1024,512]{1,0:T(8,128)(2,1)}, f32[2,512]{1,0:T(2,128)}, /*index=5*/f32[128,1024]{1,0:T(8,128)}) custom-call(bf16[1024,512]{1,0:T(8,128)(2,1)} %x_ref.1, bf16[1024,512]{1,0:T(8,128)(2,1)} %q_ref.1, bf16[1024,512]{1,0:T(8,128)(2,1)} %k_ref.1, ...), custom_call_target="tpu_custom_call" | custom-call | tf_op jit(solution)/shard_map/pallas_call | solution.py:520
  155.1 0.0 copy-start.2
  155.1 2.4 %copy.18 = bf16[1024,512]{1,0:T(8,128)(2,1)} copy(bf16[1024,512]{1,0:T(8,128)(2,1)} %get-tuple-element.12) | data formatting | bytes 2097152
  157.5 0.0 copy-done.2
  157.5 0.0 copy-start.1
  157.5 1.0 copy.19
  158.5 0.6 copy-done.1
  159.1 0.0 copy-start
  159.1 1.0 copy.20
  160.1 0.6 copy-done
  160.7 0.0 copy-start.4
  160.7 0.0 copy-start.3
  160.7 1.0 copy.21
  161.7 0.0 copy-done.4
  161.7 0.6 copy.22
  162.3 0.0 copy-done.3
  162.3 0.8 copy.23
Async XLA Ops:
  155.1 2.4 %copy-start.2 = (bf16[1024,512]{1,0:T(8,128)(2,1)S(1)}, bf16[1024,512]{1,0:T(8,128)(2,1)}, u32[]{:S(2)}) copy-start(bf16[1024,512]{1,0:T(8,128)(2,1)} %get-tuple-element.13) | copy-start | bytes 3145732
  157.5 1.6 copy-start.1
  159.1 1.6 copy-start
  160.7 1.0 copy-start.4
  160.7 1.6 copy-start.3

commit v2 on v1

--- a/solution.py
+++ b/solution.py
@@ -53,18 +53,26 @@
 
 
 def kernel(
-    x_ref,
+    x_hbm,
+    q_hbm,
+    k_hbm,
+    v_hbm,
+    taps_ref,
+    g_hbm,
+    mixed_out_hbm,
+    grad_query_hbm,
+    grad_key_hbm,
+    grad_value_hbm,
+    filter_grad_ref,
+    weight_grad_ref,
     q_ref,
     k_ref,
     v_ref,
-    taps_ref,
     g_ref,
     mixed_out_ref,
     grad_query_ref,
     grad_key_ref,
     grad_value_ref,
-    filter_grad_ref,
-    weight_grad_ref,
     mixed_send,
     up_send,
     taps_send,
@@ -97,6 +105,8 @@
     r_recv_sem,
     z_send_sem,
     z_recv_sem,
+    in_sem,
+    out_sem,
 ):
     me = lax.axis_index("seq")
     chan = lax.axis_index("chan")
@@ -104,6 +114,33 @@
     iz = lax.rem(me // 4, 2)
     iy = lax.rem(me, 4)
     sems = (send_sem, recv_sem)
+
+    own_x = pl.ds(chan * 8, 8)
+    loads = [
+        pltpu.make_async_copy(src, dst, in_sem.at[slot])
+        for slot, (src, dst) in enumerate(
+            (
+                (k_hbm, k_ref),
+                (v_hbm, v_ref),
+                (g_hbm, g_ref),
+                (q_hbm, q_ref),
+                (x_hbm, x_all.at[own_x]),
+            )
+        )
+    ]
+    for load in loads:
+        load.start()
+    stores = [
+        pltpu.make_async_copy(src, dst, out_sem.at[slot])
+        for slot, (src, dst) in enumerate(
+            (
+                (mixed_out_ref, mixed_out_hbm),
+                (grad_query_ref, grad_query_hbm),
+                (grad_key_ref, grad_key_hbm),
+                (grad_value_ref, grad_value_hbm),
+            )
+        )
+    ]
 
     barrier = pltpu.get_barrier_semaphore()
     for_peers(
@@ -133,6 +170,8 @@
         for c in range(4):
             taps_send[g, c : c + 1, :] = taps_ref[g : g + 1, c * 128 : (c + 1) * 128]
         taps_send[g, 4:8, :] = jnp.zeros((4, 128), F32)
+    loads[0].wait()
+    loads[1].wait()
     loop(ROWS // 128, make_mixed)
     pl.semaphore_wait(barrier, N + 1)
 
@@ -198,10 +237,28 @@
 
         for_peers(me, one)
 
+    near_x = pl.ds(near_peer * 8, 8)
+
+    def x_copy(slot, src, rows, peer):
+        return pltpu.make_async_remote_copy(
+            src_ref=src,
+            dst_ref=x_all.at[rows],
+            send_sem=x_send_sem.at[slot],
+            recv_sem=x_recv_sem.at[slot],
+            device_id={"chan": peer},
+            device_id_type=MESH,
+        )
+
+    x_core = x_copy(0, x_hbm, own_x, core_peer)
+    x_near = x_copy(1, x_hbm, own_x, near_peer)
+    x_pass = x_copy(2, x_all.at[near_x], near_x, core_peer)
+
     for_peers(me, lambda peer: taps_copy(peer).start())
     for_peers(me, lambda peer: mixed_copy(peer).start())
+    x_core.start()
+    loads[2].wait()
+    loads[3].wait()
     loop(ROWS // 128, make_up)
-    for_peers(me, lambda peer: up_copy(peer).start())
 
     taps_all[me] = taps_send[me // 16]
     mixed_all[pl.ds(PAD + 2 * me, 2)] = mixed_send[:, chan_rows(me), :]
@@ -220,21 +277,25 @@
         )
         return pltpu.roll(jnp.broadcast_to(wide, (B, B)), 0, 1, stride=1, stride_axis=0)
 
-    acc[...] = jnp.zeros((B, B), F32)
+    acc[:B] = jnp.zeros((B, B), F32)
 
     def make_tiles(s):
         for half in range(2):
             now = sheared(s, half)
-            toeplitz[2 * s + half] = jnp.where(col_id >= row_id, now, acc[...]).astype(BF16)
-            acc[...] = now
+            toeplitz[2 * s + half] = jnp.where(col_id >= row_id, now, acc[:B]).astype(BF16)
+            acc[:B] = now
 
     loop(N, make_tiles)
 
+    for_peers(me, lambda peer: mixed_copy(peer).wait_send())
+    for_peers(me, lambda peer: up_copy(peer).start())
+    x_near.start()
+
     wait_all(MIXED, lambda peer: mixed_all.at[pl.ds(PAD + 2 * peer, 2)], mixed_send.at[:, :CH, :])
 
     def hand_back(i, copy, send, dest):
-        for r in range(4):
-            peer = 4 * i + r
+        for r in range(8):
+            peer = 8 * i + r
 
             @pl.when(peer != me)
             def _():
@@ -245,65 +306,54 @@
                 dest[:, chan_rows(me), :] = send[pl.ds(2 * me, 2)]
 
     def conv_chunk(step):
-        i = lax.rem(me // 4 + step, 8)
-        acc[...] = jnp.zeros((B, B), F32)
-
-        def some(j):
+        i = lax.rem(ix + step, 4)
+        acc[...] = jnp.zeros((2 * B, B), F32)
+
+        def some(j, first, blocks):
             part = None
             for u in range(8):
                 m = 8 * j + u
-                lhs = mixed_all[pl.ds(PAD + 8 * i - m, 8)].reshape(B, B)
+                lhs = mixed_all[pl.ds(PAD + first - m, blocks)].reshape(blocks * CH, B)
                 term = jnp.dot(lhs, toeplitz[m], preferred_element_type=F32)
                 part = term if part is None else part + term
-            acc[...] += part
-
-        loop(i + 1, some)
-        conv_send[pl.ds(8 * i, 8)] = acc[...].astype(BF16).reshape(8, CH, B)
+            return part
+
+        def full(j):
+            acc[...] += some(j, 16 * i, 16)
+
+        loop(2 * i + 1, full)
+        acc[B:] += some(2 * i + 1, 16 * i + 8, 8)
+        conv_send[pl.ds(16 * i, 16)] = acc[...].astype(BF16).reshape(16, CH, B)
         hand_back(i, conv_copy, conv_send, conv_all)
 
-    own_x = pl.ds(pl.multiple_of(chan * ROWS, ROWS), ROWS)
-    near_x = pl.ds(pl.multiple_of(near_peer * ROWS, ROWS), ROWS)
-
-    def x_copy(slot, src, rows, peer):
-        return pltpu.make_async_remote_copy(
-            src_ref=src,
-            dst_ref=x_all.at[rows, :],
-            send_sem=x_send_sem.at[slot],
-            recv_sem=x_recv_sem.at[slot],
-            device_id={"chan": peer},
-            device_id_type=MESH,
-        )
-
-    x_core = x_copy(0, x_ref, own_x, core_peer)
-    x_near = x_copy(1, x_ref, own_x, near_peer)
-    x_pass = x_copy(2, x_all.at[near_x, :], near_x, core_peer)
-    x_core.start()
-    x_near.start()
-    x_all[own_x, :] = x_ref[...]
-    loop(8, conv_chunk)
+    loop(4, conv_chunk)
 
     wait_all(UP, lambda peer: up_all.at[pl.ds(2 * peer, 2)], up_send.at[:, :CH, :])
 
     def back_chunk(step):
-        i = lax.rem(me // 4 + step, 8)
-        acc[...] = jnp.zeros((B, B), F32)
-
-        def some(j):
+        i = lax.rem(ix + step, 4)
+        acc[...] = jnp.zeros((2 * B, B), F32)
+
+        def some(j, blocks):
             part = None
             for u in range(8):
                 m = 8 * j + u
-                lhs = up_all[pl.ds(8 * i + m, 8)].reshape(B, B)
+                lhs = up_all[pl.ds(16 * i + m, blocks)].reshape(blocks * CH, B)
                 term = lax.dot_general(
                     lhs, toeplitz[m], (((1,), (1,)), ((), ())), preferred_element_type=F32
                 )
                 part = term if part is None else part + term
-            acc[...] += part
-
-        loop(8 - i, some)
-        back_send[pl.ds(8 * i, 8)] = acc[...].astype(BF16).reshape(8, CH, B)
+            return part
+
+        def full(j):
+            acc[...] += some(j, 16)
+
+        loop(7 - 2 * i, full)
+        acc[:B] += some(7 - 2 * i, 8)
+        back_send[pl.ds(16 * i, 16)] = acc[...].astype(BF16).reshape(16, CH, B)
         hand_back(i, back_copy, back_send, back_all)
 
-    loop(8, back_chunk)
+    loop(4, back_chunk)
     x_near.wait_recv()
     x_pass.start()
 
@@ -318,26 +368,27 @@
             mixed_out_ref[rows, cols] = (q_ref[rows, cols].astype(F32) * conv).astype(BF16)
 
     loop(ROWS // 128, use_conv)
+    stores[0].start()
+    stores[1].start()
+    loads[4].wait()
     x_core.wait_recv()
     x_pass.wait_recv()
 
-    def weight_share(r):
-        px, pz = r // 2, lax.rem(r, 2)
-        rows = pl.ds(pl.multiple_of(r * 512, 512), 512)
-        for half in range(2):
-            share = lax.dot_general(
-                x_all[rows, :],
-                grad_query_ref[half * 512 : (half + 1) * 512, :],
-                (((1,), (1,)), ((), ())),
-                preferred_element_type=F32,
-            ).astype(BF16)
-            if half == 0:
-                part_a[px, pz] = share.reshape(4, 128, 512)
-            else:
-                for py in range(4):
-                    part_b[py, pz, px] = share[py * 128 : (py + 1) * 128, :]
-
-    loop(8, weight_share)
+    def share(lhs, half):
+        return lax.dot_general(
+            lhs,
+            grad_query_ref[half * 512 : (half + 1) * 512, :],
+            (((1,), (1,)), ((), ())),
+            preferred_element_type=F32,
+        ).astype(BF16)
+
+    def share_a(px, pz):
+        lhs = x_all[pl.ds(8 * px + 4 * pz, 4)].reshape(512, T)
+        part_a[px, pz] = share(lhs, 0).reshape(4, 128, 512)
+
+    def share_b(py, pz):
+        lhs = jnp.concatenate([x_all[8 * px + 4 * pz + py] for px in range(4)], axis=0)
+        part_b[py, pz] = share(lhs, 1).reshape(4, 128, 512)
 
     def x_peer(d):
         return lax.rem(ix + d, 4) * 8 + iz * 4 + iy
@@ -366,8 +417,8 @@
             ring_copy(half, stage, 5, part.at[down, 1], inbox.at[5], peer_of(3)),
         )
 
-    def ring_start(copies):
-        for c in copies[:4]:
+    def ring_start(copies, first=0, last=4):
+        for c in copies[first:last]:
             c.start()
 
     def ring_middle(copies, part, inbox, index, blocks):
@@ -402,8 +453,19 @@
     firsts = []
     for half, (part, index, peer_of, _, _) in enumerate(halves):
         copies = ring_copies(half, 0, part, first_in.at[half], index, peer_of)
-        ring_start(copies)
         firsts.append(copies)
+
+    shares = ((share_a, ix), (share_b, iy))
+    for half, (make, index) in enumerate(shares):
+        loop(2, lambda z: make(lax.rem(index + 2, 4), z))
+        ring_start(firsts[half], 0, 2)
+    for half, (make, index) in enumerate(shares):
+        loop(2, lambda z: make(lax.rem(index + 3 - 2 * z, 4), z))
+        ring_start(firsts[half], 2, 4)
+    for make, index in shares:
+        loop(2, lambda z: make(lax.rem(index + 1 + 2 * z, 4), z))
+    for make, index in shares:
+        loop(2, lambda z: make(index, z))
 
     flip = (row_id + col_id == B - 1).astype(BF16)
     for c in range(8):
@@ -428,11 +490,11 @@
     def filter_some(i):
         loop(8, lambda u: filter_tile(i, 8 * i + u))
 
-    for i in range(4):
+    for i in range(2):
         filter_some(i)
     for half, (part, index, _, _, _) in enumerate(halves):
         ring_middle(firsts[half], part, first_in.at[half], index, 4)
-    for i in range(4, 8):
+    for i in range(2, 8):
         filter_some(i)
 
     filt_part[1, NB] = jnp.zeros((8, B), F32)
@@ -461,6 +523,8 @@
             grad_value_ref[rows, cols] = (k_ref[rows, cols].astype(F32) * back).astype(BF16)
 
     loop(ROWS // 128, use_back)
+    stores[2].start()
+    stores[3].start()
 
     seconds = []
     for half, (part, index, _, across, across_peer) in enumerate(halves):
@@ -507,66 +571,99 @@
         total = second_out[half, iz].astype(F32) + third_in[half].astype(F32)
         weight_grad_ref[:, half * 512 : (half + 1) * 512] = total * weight_factor
 
-    for make in (taps_copy, mixed_copy, up_copy, conv_copy, back_copy, filt_copy):
+    for store_out in stores:
+        store_out.wait()
+    for make in (taps_copy, up_copy, conv_copy, back_copy, filt_copy):
         for_peers(me, lambda peer: make(peer).wait_send())
     for c in (x_core, x_near, x_pass, *firsts[0], *firsts[1], *seconds[0], *seconds[1], *thirds):
         c.wait_send()
 
 
+def hand_over(*refs):
+    count = len(refs) // 2
+    copies = [
+        pltpu.make_async_copy(refs[c], refs[count + c], refs[2 * count].at[c])
+        for c in range(count)
+    ]
+    for c in copies:
+        c.start()
+    for c in copies:
+        c.wait()
+
+
 def per_device(layer_input, query_proj, key_proj, value_proj, filter_taps, grad_out):
     vmem = pl.BlockSpec(memory_space=pltpu.VMEM)
+    hbm = pl.BlockSpec(memory_space=pl.ANY)
     rows = jax.ShapeDtypeStruct((ROWS, T), BF16)
+    shapes = (
+        rows,
+        rows,
+        rows,
+        rows,
+        jax.ShapeDtypeStruct((2, T), F32),
+        jax.ShapeDtypeStruct((128, ROWS), F32),
+    )
+    results = pl.pallas_call(
+        kernel,
+        out_shape=shapes,
+        in_specs=[hbm] * 4 + [vmem, hbm],
+        out_specs=[hbm] * 4 + [vmem] * 2,
+        scratch_shapes=[pltpu.VMEM((ROWS, T), BF16)] * 8
+        + [
+            pltpu.VMEM((2, ROWS, B), BF16),
+            pltpu.VMEM((2, ROWS, B), BF16),
+            pltpu.VMEM((2, 8, 128), F32),
+            pltpu.VMEM((N, 8, 128), F32),
+            pltpu.VMEM((PAD + NB, CH, B), BF16),
+            pltpu.VMEM((NB + PAD, CH, B), BF16),
+            pltpu.VMEM((B, NB * CH), BF16),
+            pltpu.VMEM((NB, B, B), BF16),
+            pltpu.VMEM((2 * B, B), F32),
+            pltpu.VMEM((NB, CH, B), BF16),
+            pltpu.VMEM((NB, CH, B), BF16),
+            pltpu.VMEM((2, ROWS, B), BF16),
+            pltpu.VMEM((2, ROWS, B), BF16),
+            pltpu.VMEM((2, NB + 1, 8, B), F32),
+            pltpu.VMEM((N, 8, 128), F32),
+            pltpu.VMEM((N, 8, 128), F32),
+            pltpu.VMEM((N, 128, T), BF16),
+            pltpu.VMEM((4, 2, 4, 128, 512), BF16),
+            pltpu.VMEM((4, 2, 4, 128, 512), BF16),
+            pltpu.VMEM((2, 6, 4, 128, 512), BF16),
+            pltpu.VMEM((2, 4, 2, 1, 128, 512), BF16),
+            pltpu.VMEM((2, 6, 1, 128, 512), BF16),
+            pltpu.VMEM((2, 2, 128, 512), BF16),
+            pltpu.VMEM((2, 128, 512), BF16),
+            pltpu.SemaphoreType.DMA((KINDS, N)),
+            pltpu.SemaphoreType.DMA((KINDS, N)),
+            pltpu.SemaphoreType.DMA((3,)),
+            pltpu.SemaphoreType.DMA((3,)),
+            pltpu.SemaphoreType.DMA((2, 2, 6)),
+            pltpu.SemaphoreType.DMA((2, 2, 6)),
+            pltpu.SemaphoreType.DMA((2,)),
+            pltpu.SemaphoreType.DMA((2,)),
+            pltpu.SemaphoreType.DMA((5,)),
+            pltpu.SemaphoreType.DMA((4,)),
+        ],
+        compiler_params=pltpu.CompilerParams(
+            collective_id=0, has_side_effects=True, vmem_limit_bytes=62 * 2**20
+        ),
+    )(
+        layer_input.reshape(8, 128, T),
+        query_proj,
+        key_proj,
+        value_proj,
+        filter_taps,
+        grad_out,
+    )
     return tuple(
         pl.pallas_call(
-            kernel,
-            out_shape=(
-                rows,
-                rows,
-                rows,
-                rows,
-                jax.ShapeDtypeStruct((2, T), F32),
-                jax.ShapeDtypeStruct((128, ROWS), F32),
-            ),
-            in_specs=[vmem] * 6,
-            out_specs=[vmem] * 6,
-            scratch_shapes=[
-                pltpu.VMEM((2, ROWS, B), BF16),
-                pltpu.VMEM((2, ROWS, B), BF16),
-                pltpu.VMEM((2, 8, 128), F32),
-                pltpu.VMEM((N, 8, 128), F32),
-                pltpu.VMEM((PAD + NB, CH, B), BF16),
-                pltpu.VMEM((NB + PAD, CH, B), BF16),
-                pltpu.VMEM((B, NB * CH), BF16),
-                pltpu.VMEM((NB, B, B), BF16),
-                pltpu.VMEM((B, B), F32),
-                pltpu.VMEM((NB, CH, B), BF16),
-                pltpu.VMEM((NB, CH, B), BF16),
-                pltpu.VMEM((2, ROWS, B), BF16),
-                pltpu.VMEM((2, ROWS, B), BF16),
-                pltpu.VMEM((2, NB + 1, 8, B), F32),
-                pltpu.VMEM((N, 8, 128), F32),
-                pltpu.VMEM((N, 8, 128), F32),
-                pltpu.VMEM((4 * ROWS, T), BF16),
-                pltpu.VMEM((4, 2, 4, 128, 512), BF16),
-                pltpu.VMEM((4, 2, 4, 128, 512), BF16),
-                pltpu.VMEM((2, 6, 4, 128, 512), BF16),
-                pltpu.VMEM((2, 4, 2, 1, 128, 512), BF16),
-                pltpu.VMEM((2, 6, 1, 128, 512), BF16),
-                pltpu.VMEM((2, 2, 128, 512), BF16),
-                pltpu.VMEM((2, 128, 512), BF16),
-                pltpu.SemaphoreType.DMA((KINDS, N)),
-                pltpu.SemaphoreType.DMA((KINDS, N)),
-                pltpu.SemaphoreType.DMA((3,)),
-                pltpu.SemaphoreType.DMA((3,)),
-                pltpu.SemaphoreType.DMA((2, 2, 6)),
-                pltpu.SemaphoreType.DMA((2, 2, 6)),
-                pltpu.SemaphoreType.DMA((2,)),
-                pltpu.SemaphoreType.DMA((2,)),
-            ],
-            compiler_params=pltpu.CompilerParams(
-                collective_id=0, has_side_effects=True, vmem_limit_bytes=60 * 2**20
-            ),
-        )(layer_input, query_proj, key_proj, value_proj, filter_taps, grad_out)
+            hand_over,
+            out_shape=shapes,
+            in_specs=[hbm] * 6,
+            out_specs=[hbm] * 6,
+            scratch_shapes=[pltpu.SemaphoreType.DMA((6,))],
+        )(*results)
     )
 
 

time: 163 us -> 293 us (1.80)
  Pallas kernels: 154 us -> 292 us
  local copies, waits for them, and re-layouts: 7.92 us -> 0 us
    pallas_call x1 -> x2, Pallas kernels: 154 us -> 292 us  [the longest x1 147 us: per_device(): pl.pallas_call(kernel, out_shape=shapes, in_specs=[hbm] * 4 + [vmem, hbm]...]
    unnamed x16 -> x0, local copies, waits for them, and re-layouts: 7.92 us -> none
where the time goes in v2:
time: 293 us; the launch traced here: 292 us
  Pallas kernels  292 us (100%)
    pallas_call x1, Pallas kernels, per_device(): pl.pallas_call(kernel, out_shape=shapes, in_specs=[hbm] * 4 + [vmem, hbm]...  147 us
    pallas_call x1, Pallas kernels, per_device(): pl.pallas_call(hand_over, out_shape=shapes, in_specs=[hbm] * 6, out_specs...  144 us

profile of v2, /device:TPU:0, one launch (start us, length us, event | category | flops | bytes accessed | tf_op | source)
XLA Modules:
  0.0 292.2 jit_solution(18338594276662127292)
XLA Ops:
  0.6 147.4 %shard_map.109 = (bf16[1024,512]{1,0:T(8,128)(2,1)}, bf16[1024,512]{1,0:T(8,128)(2,1)}, bf16[1024,512]{1,0:T(8,128)(2,1)}, bf16[1024,512]{1,0:T(8,128)(2,1)}, f32[2,512]{1,0:T(2,128)}, /*index=5*/f32[128,1024]{1,0:T(8,128)}) custom-call(bf16[8,128,512]{2,1,0:T(8,128)(2,1)} %bitcast.1, bf16[1024,512]{1,0:T(8,128)(2,1)} %q_hbm.1, bf16[1024,512]{1,0:T(8,128)(2,1)} %k_hbm.1, ...), custom_call_target="tpu_custom_call" | custom-call | tf_op jit(solution)/shard_map/pallas_call | solution.py:606
  148.0 144.2 %shard_map.110 = (bf16[1024,512]{1,0:T(8,128)(2,1)}, bf16[1024,512]{1,0:T(8,128)(2,1)}, bf16[1024,512]{1,0:T(8,128)(2,1)}, bf16[1024,512]{1,0:T(8,128)(2,1)}, f32[2,512]{1,0:T(2,128)}, /*index=5*/f32[128,1024]{1,0:T(8,128)}) custom-call(bf16[1024,512]{1,0:T(8,128)(2,1)} %get-tuple-element.12.refs_0_, bf16[1024,512]{1,0:T(8,128)(2,1)} %get-tuple-element.13.refs_1_, ...), custom_call_target="tpu_custom_call" | custom-call | tf_op jit(solution)/shard_map/pallas_call | solution.py:660

commit v3 on v2

--- a/solution.py
+++ b/solution.py
@@ -580,15 +580,18 @@
 
 
 def hand_over(*refs):
-    count = len(refs) // 2
-    copies = [
-        pltpu.make_async_copy(refs[c], refs[count + c], refs[2 * count].at[c])
-        for c in range(count)
-    ]
-    for c in copies:
-        c.start()
-    for c in copies:
-        c.wait()
+    count = len(refs) // 3
+    sources, targets, held = refs[:count], refs[count : 2 * count], refs[2 * count : 3 * count]
+    sems = refs[3 * count]
+    loads = [pltpu.make_async_copy(sources[c], held[c], sems.at[0, c]) for c in range(count)]
+    stores = [pltpu.make_async_copy(held[c], targets[c], sems.at[1, c]) for c in range(count)]
+    for load in loads:
+        load.start()
+    for load, store in zip(loads, stores):
+        load.wait()
+        store.start()
+    for store in stores:
+        store.wait()
 
 
 def per_device(layer_input, query_proj, key_proj, value_proj, filter_taps, grad_out):
@@ -662,7 +665,8 @@
             out_shape=shapes,
             in_specs=[hbm] * 6,
             out_specs=[hbm] * 6,
-            scratch_shapes=[pltpu.SemaphoreType.DMA((6,))],
+            scratch_shapes=[pltpu.VMEM(shape.shape, shape.dtype) for shape in shapes]
+            + [pltpu.SemaphoreType.DMA((2, 6))],
         )(*results)
     )
 

time: 293 us -> 152 us (0.52)
  Pallas kernels: 292 us -> 151 us
    pallas_call x1, Pallas kernels: 144 us -> 3.66 us  [per_device(): pl.pallas_call(hand_over, out_shape=shapes, in_specs=[hbm] * 6, out_specs...]
where the time goes in v3:
time: 152 us
  Pallas kernels  151 us (99%)
    pallas_call x1, Pallas kernels, per_device(): pl.pallas_call(kernel, out_shape=shapes, in_specs=[hbm] * 4 + [vmem, hbm]...  147 us
    pallas_call x1, Pallas kernels, per_device(): pl.pallas_call(hand_over, out_shape=shapes, in_specs=[hbm] * 6, out_specs...  3.66 us

profile of v3, /device:TPU:0, one launch (start us, length us, event | category | flops | bytes accessed | tf_op | source)
XLA Modules:
  0.0 151.7 jit_solution(560619879634482200)
XLA Ops:
  0.6 147.4 %shard_map.109 = (bf16[1024,512]{1,0:T(8,128)(2,1)}, bf16[1024,512]{1,0:T(8,128)(2,1)}, bf16[1024,512]{1,0:T(8,128)(2,1)}, bf16[1024,512]{1,0:T(8,128)(2,1)}, f32[2,512]{1,0:T(2,128)}, /*index=5*/f32[128,1024]{1,0:T(8,128)}) custom-call(bf16[8,128,512]{2,1,0:T(8,128)(2,1)} %bitcast.1, bf16[1024,512]{1,0:T(8,128)(2,1)} %q_hbm.1, bf16[1024,512]{1,0:T(8,128)(2,1)} %k_hbm.1, ...), custom_call_target="tpu_custom_call" | custom-call | tf_op jit(solution)/shard_map/pallas_call | solution.py:609
  148.0 3.7 %shard_map.110 = (bf16[1024,512]{1,0:T(8,128)(2,1)}, bf16[1024,512]{1,0:T(8,128)(2,1)}, bf16[1024,512]{1,0:T(8,128)(2,1)}, bf16[1024,512]{1,0:T(8,128)(2,1)}, f32[2,512]{1,0:T(2,128)}, /*index=5*/f32[128,1024]{1,0:T(8,128)}) custom-call(bf16[1024,512]{1,0:T(8,128)(2,1)} %get-tuple-element.12.refs_0_, bf16[1024,512]{1,0:T(8,128)(2,1)} %get-tuple-element.13.refs_1_, ...), custom_call_target="tpu_custom_call" | custom-call | tf_op jit(solution)/shard_map/pallas_call | solution.py:663

commit v4 on v3

--- a/solution.py
+++ b/solution.py
@@ -20,6 +20,8 @@
 NB = N * T // B
 PAD = 8
 ROWS = N * CH
+WA = 384
+WB = ROWS - WA
 KINDS = 6
 MIXED, UP, TAPS, CONV, BACK, FILT = range(KINDS)
 
@@ -92,11 +94,16 @@
     x_all,
     part_a,
     part_b,
-    first_in,
-    first_out,
-    second_in,
-    second_out,
-    third_in,
+    first_in_a,
+    first_in_b,
+    first_out_a,
+    first_out_b,
+    second_in_a,
+    second_in_b,
+    second_out_a,
+    second_out_b,
+    third_in_a,
+    third_in_b,
     send_sem,
     recv_sem,
     x_send_sem,
@@ -289,7 +296,6 @@
 
     for_peers(me, lambda peer: mixed_copy(peer).wait_send())
     for_peers(me, lambda peer: up_copy(peer).start())
-    x_near.start()
 
     wait_all(MIXED, lambda peer: mixed_all.at[pl.ds(PAD + 2 * peer, 2)], mixed_send.at[:, :CH, :])
 
@@ -327,6 +333,7 @@
         hand_back(i, conv_copy, conv_send, conv_all)
 
     loop(4, conv_chunk)
+    x_near.start()
 
     wait_all(UP, lambda peer: up_all.at[pl.ds(2 * peer, 2)], up_send.at[:, :CH, :])
 
@@ -351,11 +358,8 @@
         loop(7 - 2 * i, full)
         acc[:B] += some(7 - 2 * i, 8)
         back_send[pl.ds(16 * i, 16)] = acc[...].astype(BF16).reshape(16, CH, B)
-        hand_back(i, back_copy, back_send, back_all)
 
     loop(4, back_chunk)
-    x_near.wait_recv()
-    x_pass.start()
 
     wait_all(CONV, lambda peer: conv_all.at[:, chan_rows(peer), :], conv_send.at[:2])
 
@@ -372,23 +376,22 @@
     stores[1].start()
     loads[4].wait()
     x_core.wait_recv()
-    x_pass.wait_recv()
-
-    def share(lhs, half):
+
+    def share(lhs, first, count):
         return lax.dot_general(
             lhs,
-            grad_query_ref[half * 512 : (half + 1) * 512, :],
+            grad_query_ref[first : first + count, :],
             (((1,), (1,)), ((), ())),
             preferred_element_type=F32,
         ).astype(BF16)
 
     def share_a(px, pz):
         lhs = x_all[pl.ds(8 * px + 4 * pz, 4)].reshape(512, T)
-        part_a[px, pz] = share(lhs, 0).reshape(4, 128, 512)
-
-    def share_b(py, pz):
-        lhs = jnp.concatenate([x_all[8 * px + 4 * pz + py] for px in range(4)], axis=0)
-        part_b[py, pz] = share(lhs, 1).reshape(4, 128, 512)
+        part_a[px, pz] = share(lhs, 0, WA).reshape(4, 128, WA)
+
+    def share_b(py, pz, pair):
+        lhs = jnp.concatenate([x_all[16 * pair + 8 * e + 4 * pz + py] for e in range(2)], axis=0)
+        part_b[py, pz, pl.ds(2 * pair, 2)] = share(lhs, WA, WB).reshape(2, 128, WB)
 
     def x_peer(d):
         return lax.rem(ix + d, 4) * 8 + iz * 4 + iy
@@ -396,76 +399,81 @@
     def y_peer(d):
         return ix * 8 + iz * 4 + lax.rem(iy + d, 4)
 
-    def ring_copy(half, stage, slot, src, dst, peer):
-        return pltpu.make_async_remote_copy(
-            src_ref=src,
-            dst_ref=dst,
-            send_sem=r_send_sem.at[half, stage, slot],
-            recv_sem=r_recv_sem.at[half, stage, slot],
-            device_id={"seq": peer},
-            device_id_type=MESH,
-        )
-
-    def ring_copies(half, stage, part, inbox, index, peer_of):
+    def ring_copies(bank, view, inbox, index, peer_of):
         up, down, far = (lax.rem(index + d, 4) for d in (1, 3, 2))
+
+        def ring_copy(slot, target, side, hop):
+            return pltpu.make_async_remote_copy(
+                src_ref=view(target, side),
+                dst_ref=inbox.at[slot],
+                send_sem=r_send_sem.at[bank, slot],
+                recv_sem=r_recv_sem.at[bank, slot],
+                device_id={"seq": peer_of(hop)},
+                device_id_type=MESH,
+            )
+
         return (
-            ring_copy(half, stage, 0, part.at[far, 0], inbox.at[0], peer_of(1)),
-            ring_copy(half, stage, 1, part.at[far, 1], inbox.at[1], peer_of(3)),
-            ring_copy(half, stage, 2, part.at[up, 1], inbox.at[2], peer_of(1)),
-            ring_copy(half, stage, 3, part.at[down, 0], inbox.at[3], peer_of(3)),
-            ring_copy(half, stage, 4, part.at[up, 0], inbox.at[4], peer_of(1)),
-            ring_copy(half, stage, 5, part.at[down, 1], inbox.at[5], peer_of(3)),
+            ring_copy(0, far, 0, 1),
+            ring_copy(1, far, 1, 3),
+            ring_copy(2, up, 1, 1),
+            ring_copy(3, down, 0, 3),
+            ring_copy(4, up, 0, 1),
+            ring_copy(5, down, 1, 3),
         )
 
     def ring_start(copies, first=0, last=4):
         for c in copies[first:last]:
             c.start()
 
-    def ring_middle(copies, part, inbox, index, blocks):
+    def ring_middle(copies, view, inbox, index, blocks):
         for slot, there, side in ((0, 1, 0), (1, 3, 1)):
             copies[slot].wait_recv()
-            target = lax.rem(index + there, 4)
+            held = view(lax.rem(index + there, 4), side)
 
             def add(e):
-                total = part[target, side, e].astype(F32) + inbox[slot, e].astype(F32)
-                part[target, side, e] = total.astype(BF16)
+                total = held[e].astype(F32) + inbox[slot, e].astype(F32)
+                held[e] = total.astype(BF16)
 
             loop(blocks, add)
             copies[4 + slot].start()
 
-    def ring_end(copies, part, inbox, index, blocks, store):
+    def ring_end(copies, view, inbox, index, blocks, store):
         for slot in (2, 3, 4, 5):
             copies[slot].wait_recv()
 
         def add(e):
             for side, one, two in ((0, 4, 3), (1, 5, 2)):
-                total = part[index, side, e].astype(F32) + (
+                total = view(index, side)[e].astype(F32) + (
                     inbox[one, e].astype(F32) + inbox[two, e].astype(F32)
                 )
                 store(side, e, total)
 
         loop(blocks, add)
 
-    halves = (
-        (part_a, ix, x_peer, iy, y_peer),
-        (part_b, iy, y_peer, ix, x_peer),
-    )
-    firsts = []
-    for half, (part, index, peer_of, _, _) in enumerate(halves):
-        copies = ring_copies(half, 0, part, first_in.at[half], index, peer_of)
-        firsts.append(copies)
-
-    shares = ((share_a, ix), (share_b, iy))
-    for half, (make, index) in enumerate(shares):
-        loop(2, lambda z: make(lax.rem(index + 2, 4), z))
-        ring_start(firsts[half], 0, 2)
-    for half, (make, index) in enumerate(shares):
-        loop(2, lambda z: make(lax.rem(index + 3 - 2 * z, 4), z))
-        ring_start(firsts[half], 2, 4)
-    for make, index in shares:
-        loop(2, lambda z: make(lax.rem(index + 1 + 2 * z, 4), z))
-    for make, index in shares:
-        loop(2, lambda z: make(index, z))
+    def view_a(target, side):
+        return part_a.at[target, side]
+
+    def view_b(pair):
+        return lambda target, side: part_b.at[target, side, pl.ds(2 * pair, 2)]
+
+    here = chan // 2
+    there = 1 - here
+    ring_a = (view_a, first_in_a, ix)
+    ring_b0 = (view_b(here), first_in_b.at[0], iy)
+    ring_b1 = (view_b(there), first_in_b.at[1], iy)
+    copies_a = ring_copies(0, *ring_a, x_peer)
+    copies_b0 = ring_copies(1, *ring_b0, y_peer)
+    copies_b1 = ring_copies(2, *ring_b1, y_peer)
+
+    def shares_b(copies, pair):
+        loop(2, lambda z: share_b(lax.rem(iy + 2, 4), z, pair))
+        ring_start(copies, 0, 2)
+        loop(2, lambda z: share_b(lax.rem(iy + 3 - 2 * z, 4), z, pair))
+        ring_start(copies, 2, 4)
+        loop(2, lambda z: share_b(lax.rem(iy + 1 + 2 * z, 4), z, pair))
+
+    shares_b(copies_b0, here)
+    loop(2, lambda z: share_b(iy, z, here))
 
     flip = (row_id + col_id == B - 1).astype(BF16)
     for c in range(8):
@@ -490,11 +498,28 @@
     def filter_some(i):
         loop(8, lambda u: filter_tile(i, 8 * i + u))
 
-    for i in range(2):
-        filter_some(i)
-    for half, (part, index, _, _, _) in enumerate(halves):
-        ring_middle(firsts[half], part, first_in.at[half], index, 4)
-    for i in range(2, 8):
+    filter_some(0)
+    ring_middle(copies_b0, *ring_b0, 2)
+
+    x_near.wait_recv()
+    x_pass.start()
+    filter_some(7)
+    filter_some(6)
+    x_pass.wait_recv()
+    loop(2, lambda z: share_a(lax.rem(ix + 2, 4), z))
+    ring_start(copies_a, 0, 2)
+    loop(2, lambda z: share_a(lax.rem(ix + 3 - 2 * z, 4), z))
+    ring_start(copies_a, 2, 4)
+    loop(2, lambda z: share_a(lax.rem(ix + 1 + 2 * z, 4), z))
+    shares_b(copies_b1, there)
+    for_peers(me, lambda peer: back_copy(peer).start())
+    back_all[:, chan_rows(me), :] = back_send[pl.ds(2 * me, 2)]
+    loop(2, lambda z: share_a(ix, z))
+    loop(2, lambda z: share_b(iy, z, there))
+    filter_some(1)
+    ring_middle(copies_a, *ring_a, 4)
+    ring_middle(copies_b1, *ring_b1, 2)
+    for i in range(2, 6):
         filter_some(i)
 
     filt_part[1, NB] = jnp.zeros((8, B), F32)
@@ -526,20 +551,30 @@
     stores[2].start()
     stores[3].start()
 
-    seconds = []
-    for half, (part, index, _, across, across_peer) in enumerate(halves):
-
+    def second_view(held):
+        return lambda target, side: held.at[target, side]
+
+    ring_c = (second_view(first_out_a), second_in_a, iy)
+    ring_d = (second_view(first_out_b), second_in_b, ix)
+    copies_c = ring_copies(3, *ring_c, y_peer)
+    copies_d = ring_copies(4, *ring_d, x_peer)
+
+    def store_a(side, e, total):
+        first_out_a[e, side, 0] = total.astype(BF16)
+
+    def store_b(pair):
         def store(side, e, total):
-            first_out[half, e, side, 0] = total.astype(BF16)
-
-        ring_end(firsts[half], part, first_in.at[half], index, 4, store)
-        copies = ring_copies(
-            half, 1, first_out.at[half], second_in.at[half], across, across_peer
-        )
-        ring_start(copies)
-        seconds.append(copies)
-    for half, (_, _, _, across, _) in enumerate(halves):
-        ring_middle(seconds[half], first_out.at[half], second_in.at[half], across, 1)
+            first_out_b[2 * pair + e, side, 0] = total.astype(BF16)
+
+        return store
+
+    ring_end(copies_b0, *ring_b0, 2, store_b(here))
+    ring_end(copies_b1, *ring_b1, 2, store_b(there))
+    ring_start(copies_d)
+    ring_end(copies_a, *ring_a, 4, store_a)
+    ring_start(copies_c)
+    ring_middle(copies_d, *ring_d, 1)
+    ring_middle(copies_c, *ring_c, 1)
 
     wait_all(FILT, lambda peer: filt_all.at[peer], filt_send.at[0])
     for g in range(2):
@@ -547,35 +582,44 @@
         for c in range(4):
             filter_grad_ref[g : g + 1, c * 128 : (c + 1) * 128] = total[c : c + 1, :]
 
-    thirds = []
     other = ix * 8 + (1 - iz) * 4 + iy
-    for half, (_, _, _, across, _) in enumerate(halves):
-
-        def keep(side, e, total):
-            second_out[half, side] = total.astype(BF16)
-
-        ring_end(seconds[half], first_out.at[half], second_in.at[half], across, 1, keep)
-        copy = pltpu.make_async_remote_copy(
-            src_ref=second_out.at[half, 1 - iz],
-            dst_ref=third_in.at[half],
-            send_sem=z_send_sem.at[half],
-            recv_sem=z_recv_sem.at[half],
+
+    def z_copy(slot, held, inbox):
+        return pltpu.make_async_remote_copy(
+            src_ref=held.at[1 - iz],
+            dst_ref=inbox,
+            send_sem=z_send_sem.at[slot],
+            recv_sem=z_recv_sem.at[slot],
             device_id={"seq": other},
             device_id_type=MESH,
         )
-        copy.start()
-        thirds.append(copy)
+
+    def keep(held):
+        def store(side, e, total):
+            held[side] = total.astype(BF16)
+
+        return store
+
+    copy_b = z_copy(1, second_out_b, third_in_b)
+    copy_a = z_copy(0, second_out_a, third_in_a)
+    ring_end(copies_d, *ring_d, 1, keep(second_out_b))
+    copy_b.start()
+    ring_end(copies_c, *ring_c, 1, keep(second_out_a))
+    copy_a.start()
     weight_factor = 1.0 / math.sqrt(N * T)
-    for half in range(2):
-        thirds[half].wait_recv()
-        total = second_out[half, iz].astype(F32) + third_in[half].astype(F32)
-        weight_grad_ref[:, half * 512 : (half + 1) * 512] = total * weight_factor
+    copy_b.wait_recv()
+    total = second_out_b[iz].astype(F32) + third_in_b[...].astype(F32)
+    weight_grad_ref[:, WA:] = total * weight_factor
+    copy_a.wait_recv()
+    total = second_out_a[iz].astype(F32) + third_in_a[...].astype(F32)
+    weight_grad_ref[:, :WA] = total * weight_factor
 
     for store_out in stores:
         store_out.wait()
     for make in (taps_copy, up_copy, conv_copy, back_copy, filt_copy):
         for_peers(me, lambda peer: make(peer).wait_send())
-    for c in (x_core, x_near, x_pass, *firsts[0], *firsts[1], *seconds[0], *seconds[1], *thirds):
+    rings = (*copies_a, *copies_b0, *copies_b1, *copies_c, *copies_d)
+    for c in (x_core, x_near, x_pass, *rings, copy_a, copy_b):
         c.wait_send()
 
 
@@ -630,19 +674,24 @@
             pltpu.VMEM((N, 8, 128), F32),
             pltpu.VMEM((N, 8, 128), F32),
             pltpu.VMEM((N, 128, T), BF16),
-            pltpu.VMEM((4, 2, 4, 128, 512), BF16),
-            pltpu.VMEM((4, 2, 4, 128, 512), BF16),
-            pltpu.VMEM((2, 6, 4, 128, 512), BF16),
-            pltpu.VMEM((2, 4, 2, 1, 128, 512), BF16),
-            pltpu.VMEM((2, 6, 1, 128, 512), BF16),
-            pltpu.VMEM((2, 2, 128, 512), BF16),
-            pltpu.VMEM((2, 128, 512), BF16),
+            pltpu.VMEM((4, 2, 4, 128, WA), BF16),
+            pltpu.VMEM((4, 2, 4, 128, WB), BF16),
+            pltpu.VMEM((6, 4, 128, WA), BF16),
+            pltpu.VMEM((2, 6, 2, 128, WB), BF16),
+            pltpu.VMEM((4, 2, 1, 128, WA), BF16),
+            pltpu.VMEM((4, 2, 1, 128, WB), BF16),
+            pltpu.VMEM((6, 1, 128, WA), BF16),
+            pltpu.VMEM((6, 1, 128, WB), BF16),
+            pltpu.VMEM((2, 128, WA), BF16),
+            pltpu.VMEM((2, 128, WB), BF16),
+            pltpu.VMEM((128, WA), BF16),
+            pltpu.VMEM((128, WB), BF16),
             pltpu.SemaphoreType.DMA((KINDS, N)),
             pltpu.SemaphoreType.DMA((KINDS, N)),
             pltpu.SemaphoreType.DMA((3,)),
             pltpu.SemaphoreType.DMA((3,)),
-            pltpu.SemaphoreType.DMA((2, 2, 6)),
-            pltpu.SemaphoreType.DMA((2, 2, 6)),
+            pltpu.SemaphoreType.DMA((5, 6)),
+            pltpu.SemaphoreType.DMA((5, 6)),
             pltpu.SemaphoreType.DMA((2,)),
             pltpu.SemaphoreType.DMA((2,)),
             pltpu.SemaphoreType.DMA((5,)),

time: 152 us -> 147 us (0.967)
  Pallas kernels: 151 us -> 145 us
    pallas_call x1, Pallas kernels: 147 us -> 141 us  [per_device(): pl.pallas_call(kernel, out_shape=shapes, in_specs=[hbm] * 4 + [vmem, hbm]...]
where the time goes in v4:
time: 147 us; the launch traced here: 146 us
  Pallas kernels  145 us (99%)
    pallas_call x1, Pallas kernels, per_device(): pl.pallas_call(kernel, out_shape=shapes, in_specs=[hbm] * 4 + [vmem, hbm]...  141 us
    pallas_call x1, Pallas kernels, per_device(): pl.pallas_call(hand_over, out_shape=shapes, in_specs=[hbm] * 6, out_specs...  3.66 us

profile of v4, /device:TPU:0, one launch (start us, length us, event | category | flops | bytes accessed | tf_op | source)
XLA Modules:
  0.0 145.7 jit_solution(13288942853047043600)
XLA Ops:
  0.6 141.4 %shard_map.109 = (bf16[1024,512]{1,0:T(8,128)(2,1)}, bf16[1024,512]{1,0:T(8,128)(2,1)}, bf16[1024,512]{1,0:T(8,128)(2,1)}, bf16[1024,512]{1,0:T(8,128)(2,1)}, f32[2,512]{1,0:T(2,128)}, /*index=5*/f32[128,1024]{1,0:T(8,128)}) custom-call(bf16[8,128,512]{2,1,0:T(8,128)(2,1)} %bitcast.1, bf16[1024,512]{1,0:T(8,128)(2,1)} %q_hbm.1, bf16[1024,512]{1,0:T(8,128)(2,1)} %k_hbm.1, ...), custom_call_target="tpu_custom_call" | custom-call | tf_op jit(solution)/shard_map/pallas_call | solution.py:653
  142.1 3.7 %shard_map.110 = (bf16[1024,512]{1,0:T(8,128)(2,1)}, bf16[1024,512]{1,0:T(8,128)(2,1)}, bf16[1024,512]{1,0:T(8,128)(2,1)}, bf16[1024,512]{1,0:T(8,128)(2,1)}, f32[2,512]{1,0:T(2,128)}, /*index=5*/f32[128,1024]{1,0:T(8,128)}) custom-call(bf16[1024,512]{1,0:T(8,128)(2,1)} %get-tuple-element.12.refs_0_, bf16[1024,512]{1,0:T(8,128)(2,1)} %get-tuple-element.13.refs_1_, ...), custom_call_target="tpu_custom_call" | custom-call | tf_op jit(solution)/shard_map/pallas_call | solution.py:712

commit v5 on v4

--- a/solution.py
+++ b/solution.py
@@ -273,6 +273,9 @@
     mixed_all[:PAD] = jnp.zeros((PAD, CH, B), BF16)
     up_all[NB:] = jnp.zeros((PAD, CH, B), BF16)
 
+    for_peers(me, lambda peer: mixed_copy(peer).wait_send())
+    x_near.start()
+
     wait_all(TAPS, lambda peer: taps_all.at[peer], taps_send.at[0])
     row_id = lax.broadcasted_iota(jnp.int32, (B, B), 0)
     col_id = lax.broadcasted_iota(jnp.int32, (B, B), 1)
@@ -293,9 +296,6 @@
             acc[:B] = now
 
     loop(N, make_tiles)
-
-    for_peers(me, lambda peer: mixed_copy(peer).wait_send())
-    for_peers(me, lambda peer: up_copy(peer).start())
 
     wait_all(MIXED, lambda peer: mixed_all.at[pl.ds(PAD + 2 * peer, 2)], mixed_send.at[:, :CH, :])
 
@@ -333,7 +333,146 @@
         hand_back(i, conv_copy, conv_send, conv_all)
 
     loop(4, conv_chunk)
-    x_near.start()
+
+    for_peers(me, lambda peer: up_copy(peer).start())
+
+
+    wait_all(CONV, lambda peer: conv_all.at[:, chan_rows(peer), :], conv_send.at[:2])
+
+    def use_conv(r):
+        rows = pl.ds(pl.multiple_of(r * 128, 128), 128)
+        for half in range(2):
+            cols = slice(half * B, (half + 1) * B)
+            conv = conv_all[half, rows, :].astype(F32)
+            grad_query_ref[rows, cols] = (g_ref[rows, cols].astype(F32) * conv).astype(BF16)
+            mixed_out_ref[rows, cols] = (q_ref[rows, cols].astype(F32) * conv).astype(BF16)
+
+    loop(ROWS // 128, use_conv)
+    stores[0].start()
+    stores[1].start()
+    loads[4].wait()
+    x_core.wait_recv()
+
+    def share(lhs, first, count):
+        return lax.dot_general(
+            lhs,
+            grad_query_ref[first : first + count, :],
+            (((1,), (1,)), ((), ())),
+            preferred_element_type=F32,
+        ).astype(BF16)
+
+    def share_a(px, pz):
+        lhs = x_all[pl.ds(8 * px + 4 * pz, 4)].reshape(512, T)
+        part_a[px, pz] = share(lhs, 0, WA).reshape(4, 128, WA)
+
+    def share_b(py, pz, pair):
+        lhs = jnp.concatenate([x_all[16 * pair + 8 * e + 4 * pz + py] for e in range(2)], axis=0)
+        part_b[py, pz, pl.ds(2 * pair, 2)] = share(lhs, WA, WB).reshape(2, 128, WB)
+
+    def x_peer(d):
+        return lax.rem(ix + d, 4) * 8 + iz * 4 + iy
+
+    def y_peer(d):
+        return ix * 8 + iz * 4 + lax.rem(iy + d, 4)
+
+    def ring_copies(bank, view, inbox, index, peer_of):
+        up, down, far = (lax.rem(index + d, 4) for d in (1, 3, 2))
+
+        def ring_copy(slot, target, side, hop):
+            return pltpu.make_async_remote_copy(
+                src_ref=view(target, side),
+                dst_ref=inbox.at[slot],
+                send_sem=r_send_sem.at[bank, slot],
+                recv_sem=r_recv_sem.at[bank, slot],
+                device_id={"seq": peer_of(hop)},
+                device_id_type=MESH,
+            )
+
+        return (
+            ring_copy(0, far, 0, 1),
+            ring_copy(1, far, 1, 3),
+            ring_copy(2, up, 1, 1),
+            ring_copy(3, down, 0, 3),
+            ring_copy(4, up, 0, 1),
+            ring_copy(5, down, 1, 3),
+        )
+
+    def ring_start(copies, first=0, last=4):
+        for c in copies[first:last]:
+            c.start()
+
+    def ring_middle(copies, view, inbox, index, blocks):
+        for slot, there, side in ((0, 1, 0), (1, 3, 1)):
+            copies[slot].wait_recv()
+            held = view(lax.rem(index + there, 4), side)
+
+            def add(e):
+                total = held[e].astype(F32) + inbox[slot, e].astype(F32)
+                held[e] = total.astype(BF16)
+
+            loop(blocks, add)
+            copies[4 + slot].start()
+
+    def ring_end(copies, view, inbox, index, blocks, store):
+        for slot in (2, 3, 4, 5):
+            copies[slot].wait_recv()
+
+        def add(e):
+            for side, one, two in ((0, 4, 3), (1, 5, 2)):
+                total = view(index, side)[e].astype(F32) + (
+                    inbox[one, e].astype(F32) + inbox[two, e].astype(F32)
+                )
+                store(side, e, total)
+
+        loop(blocks, add)
+
+    def view_a(target, side):
+        return part_a.at[target, side]
+
+    def view_b(pair):
+        return lambda target, side: part_b.at[target, side, pl.ds(2 * pair, 2)]
+
+    here = chan // 2
+    there = 1 - here
+    ring_a = (view_a, first_in_a, ix)
+    ring_b0 = (view_b(here), first_in_b.at[0], iy)
+    ring_b1 = (view_b(there), first_in_b.at[1], iy)
+    copies_a = ring_copies(0, *ring_a, x_peer)
+    copies_b0 = ring_copies(1, *ring_b0, y_peer)
+    copies_b1 = ring_copies(2, *ring_b1, y_peer)
+
+    def shares_b(copies, pair):
+        loop(2, lambda z: share_b(lax.rem(iy + 2, 4), z, pair))
+        ring_start(copies, 0, 2)
+        loop(2, lambda z: share_b(lax.rem(iy + 3 - 2 * z, 4), z, pair))
+        ring_start(copies, 2, 4)
+        loop(2, lambda z: share_b(lax.rem(iy + 1 + 2 * z, 4), z, pair))
+
+    shares_b(copies_b0, here)
+    loop(2, lambda z: share_b(iy, z, here))
+
+    flip = (row_id + col_id == B - 1).astype(BF16)
+    for c in range(8):
+        piece = mixed_all[PAD + 8 * c : PAD + 8 * c + 8].reshape(B, B)
+        mixed_flip[:, c * B : (c + 1) * B] = lax.dot_general(
+            flip, piece, (((1,), (1,)), ((), ())), preferred_element_type=F32
+        ).astype(BF16)
+
+    def filter_tile(i, m):
+        depth = (8 - i) * B
+        corr = jnp.dot(
+            mixed_flip[:, :depth],
+            up_all[pl.ds(m, 8 * (8 - i))].reshape(depth, B),
+            preferred_element_type=F32,
+        )
+        turned = pltpu.roll(corr, 1, 1, stride=1, stride_axis=0)
+        above = jnp.where(col_id <= row_id, turned, 0.0)
+        below = turned - above
+        filt_part[0, m] = jnp.sum(above.reshape(B // 8, 8, B), axis=0)
+        filt_part[1, m] = jnp.sum(below.reshape(B // 8, 8, B), axis=0)
+
+    def filter_some(i):
+        loop(8, lambda u: filter_tile(i, 8 * i + u))
 
     wait_all(UP, lambda peer: up_all.at[pl.ds(2 * peer, 2)], up_send.at[:, :CH, :])
 
@@ -359,152 +498,13 @@
         acc[:B] += some(7 - 2 * i, 8)
         back_send[pl.ds(16 * i, 16)] = acc[...].astype(BF16).reshape(16, CH, B)
 
-    loop(4, back_chunk)
-
-    wait_all(CONV, lambda peer: conv_all.at[:, chan_rows(peer), :], conv_send.at[:2])
-
-    def use_conv(r):
-        rows = pl.ds(pl.multiple_of(r * 128, 128), 128)
-        for half in range(2):
-            cols = slice(half * B, (half + 1) * B)
-            conv = conv_all[half, rows, :].astype(F32)
-            grad_query_ref[rows, cols] = (g_ref[rows, cols].astype(F32) * conv).astype(BF16)
-            mixed_out_ref[rows, cols] = (q_ref[rows, cols].astype(F32) * conv).astype(BF16)
-
-    loop(ROWS // 128, use_conv)
-    stores[0].start()
-    stores[1].start()
-    loads[4].wait()
-    x_core.wait_recv()
-
-    def share(lhs, first, count):
-        return lax.dot_general(
-            lhs,
-            grad_query_ref[first : first + count, :],
-            (((1,), (1,)), ((), ())),
-            preferred_element_type=F32,
-        ).astype(BF16)
-
-    def share_a(px, pz):
-        lhs = x_all[pl.ds(8 * px + 4 * pz, 4)].reshape(512, T)
-        part_a[px, pz] = share(lhs, 0, WA).reshape(4, 128, WA)
-
-    def share_b(py, pz, pair):
-        lhs = jnp.concatenate([x_all[16 * pair + 8 * e + 4 * pz + py] for e in range(2)], axis=0)
-        part_b[py, pz, pl.ds(2 * pair, 2)] = share(lhs, WA, WB).reshape(2, 128, WB)
-
-    def x_peer(d):
-        return lax.rem(ix + d, 4) * 8 + iz * 4 + iy
-
-    def y_peer(d):
-        return ix * 8 + iz * 4 + lax.rem(iy + d, 4)
-
-    def ring_copies(bank, view, inbox, index, peer_of):
-        up, down, far = (lax.rem(index + d, 4) for d in (1, 3, 2))
-
-        def ring_copy(slot, target, side, hop):
-            return pltpu.make_async_remote_copy(
-                src_ref=view(target, side),
-                dst_ref=inbox.at[slot],
-                send_sem=r_send_sem.at[bank, slot],
-                recv_sem=r_recv_sem.at[bank, slot],
-                device_id={"seq": peer_of(hop)},
-                device_id_type=MESH,
-            )
-
-        return (
-            ring_copy(0, far, 0, 1),
-            ring_copy(1, far, 1, 3),
-            ring_copy(2, up, 1, 1),
-            ring_copy(3, down, 0, 3),
-            ring_copy(4, up, 0, 1),
-            ring_copy(5, down, 1, 3),
-        )
-
-    def ring_start(copies, first=0, last=4):
-        for c in copies[first:last]:
-            c.start()
-
-    def ring_middle(copies, view, inbox, index, blocks):
-        for slot, there, side in ((0, 1, 0), (1, 3, 1)):
-            copies[slot].wait_recv()
-            held = view(lax.rem(index + there, 4), side)
-
-            def add(e):
-                total = held[e].astype(F32) + inbox[slot, e].astype(F32)
-                held[e] = total.astype(BF16)
-
-            loop(blocks, add)
-            copies[4 + slot].start()
-
-    def ring_end(copies, view, inbox, index, blocks, store):
-        for slot in (2, 3, 4, 5):
-            copies[slot].wait_recv()
-
-        def add(e):
-            for side, one, two in ((0, 4, 3), (1, 5, 2)):
-                total = view(index, side)[e].astype(F32) + (
-                    inbox[one, e].astype(F32) + inbox[two, e].astype(F32)
-                )
-                store(side, e, total)
-
-        loop(blocks, add)
-
-    def view_a(target, side):
-        return part_a.at[target, side]
-
-    def view_b(pair):
-        return lambda target, side: part_b.at[target, side, pl.ds(2 * pair, 2)]
-
-    here = chan // 2
-    there = 1 - here
-    ring_a = (view_a, first_in_a, ix)
-    ring_b0 = (view_b(here), first_in_b.at[0], iy)
-    ring_b1 = (view_b(there), first_in_b.at[1], iy)
-    copies_a = ring_copies(0, *ring_a, x_peer)
-    copies_b0 = ring_copies(1, *ring_b0, y_peer)
-    copies_b1 = ring_copies(2, *ring_b1, y_peer)
-
-    def shares_b(copies, pair):
-        loop(2, lambda z: share_b(lax.rem(iy + 2, 4), z, pair))
-        ring_start(copies, 0, 2)
-        loop(2, lambda z: share_b(lax.rem(iy + 3 - 2 * z, 4), z, pair))
-        ring_start(copies, 2, 4)
-        loop(2, lambda z: share_b(lax.rem(iy + 1 + 2 * z, 4), z, pair))
-
-    shares_b(copies_b0, here)
-    loop(2, lambda z: share_b(iy, z, here))
-
-    flip = (row_id + col_id == B - 1).astype(BF16)
-    for c in range(8):
-        piece = mixed_all[PAD + 8 * c : PAD + 8 * c + 8].reshape(B, B)
-        mixed_flip[:, c * B : (c + 1) * B] = lax.dot_general(
-            flip, piece, (((1,), (1,)), ((), ())), preferred_element_type=F32
-        ).astype(BF16)
-
-    def filter_tile(i, m):
-        depth = (8 - i) * B
-        corr = jnp.dot(
-            mixed_flip[:, :depth],
-            up_all[pl.ds(m, 8 * (8 - i))].reshape(depth, B),
-            preferred_element_type=F32,
-        )
-        turned = pltpu.roll(corr, 1, 1, stride=1, stride_axis=0)
-        above = jnp.where(col_id <= row_id, turned, 0.0)
-        below = turned - above
-        filt_part[0, m] = jnp.sum(above.reshape(B // 8, 8, B), axis=0)
-        filt_part[1, m] = jnp.sum(below.reshape(B // 8, 8, B), axis=0)
-
-    def filter_some(i):
-        loop(8, lambda u: filter_tile(i, 8 * i + u))
-
-    filter_some(0)
+    loop(1, back_chunk)
     ring_middle(copies_b0, *ring_b0, 2)
+    loop(2, back_chunk, 1)
 
     x_near.wait_recv()
     x_pass.start()
-    filter_some(7)
-    filter_some(6)
+    loop(4, back_chunk, 2)
     x_pass.wait_recv()
     loop(2, lambda z: share_a(lax.rem(ix + 2, 4), z))
     ring_start(copies_a, 0, 2)
@@ -516,10 +516,10 @@
     back_all[:, chan_rows(me), :] = back_send[pl.ds(2 * me, 2)]
     loop(2, lambda z: share_a(ix, z))
     loop(2, lambda z: share_b(iy, z, there))
-    filter_some(1)
+    filter_some(0)
     ring_middle(copies_a, *ring_a, 4)
     ring_middle(copies_b1, *ring_b1, 2)
-    for i in range(2, 6):
+    for i in range(1, 8):
         filter_some(i)
 
     filt_part[1, NB] = jnp.zeros((8, B), F32)

time: 147 us -> 164 us (1.12)
  Pallas kernels: 145 us -> 163 us
    pallas_call x1, Pallas kernels: 141 us -> 159 us  [per_device(): pl.pallas_call(kernel, out_shape=shapes, in_specs=[hbm] * 4 + [vmem, hbm]...]
where the time goes in v5:
time: 164 us; the launch traced here: 163 us
  Pallas kernels  163 us (99%)
    pallas_call x1, Pallas kernels, per_device(): pl.pallas_call(kernel, out_shape=shapes, in_specs=[hbm] * 4 + [vmem, hbm]...  159 us
    pallas_call x1, Pallas kernels, per_device(): pl.pallas_call(hand_over, out_shape=shapes, in_specs=[hbm] * 6, out_specs...  3.66 us

profile of v5, /device:TPU:0, one launch (start us, length us, event | category | flops | bytes accessed | tf_op | source)
XLA Modules:
  0.0 163.5 jit_solution(14503473440255778105)
XLA Ops:
  0.6 159.2 %shard_map.109 = (bf16[1024,512]{1,0:T(8,128)(2,1)}, bf16[1024,512]{1,0:T(8,128)(2,1)}, bf16[1024,512]{1,0:T(8,128)(2,1)}, bf16[1024,512]{1,0:T(8,128)(2,1)}, f32[2,512]{1,0:T(2,128)}, /*index=5*/f32[128,1024]{1,0:T(8,128)}) custom-call(bf16[8,128,512]{2,1,0:T(8,128)(2,1)} %bitcast.1, bf16[1024,512]{1,0:T(8,128)(2,1)} %q_hbm.1, bf16[1024,512]{1,0:T(8,128)(2,1)} %k_hbm.1, ...), custom_call_target="tpu_custom_call" | custom-call | tf_op jit(solution)/shard_map/pallas_call | solution.py:653
  159.8 3.7 %shard_map.110 = (bf16[1024,512]{1,0:T(8,128)(2,1)}, bf16[1024,512]{1,0:T(8,128)(2,1)}, bf16[1024,512]{1,0:T(8,128)(2,1)}, bf16[1024,512]{1,0:T(8,128)(2,1)}, f32[2,512]{1,0:T(2,128)}, /*index=5*/f32[128,1024]{1,0:T(8,128)}) custom-call(bf16[1024,512]{1,0:T(8,128)(2,1)} %get-tuple-element.12.refs_0_, bf16[1024,512]{1,0:T(8,128)(2,1)} %get-tuple-element.13.refs_1_, ...), custom_call_target="tpu_custom_call" | custom-call | tf_op jit(solution)/shard_map/pallas_call | solution.py:712

commit v6 on v4

--- a/solution.py
+++ b/solution.py
@@ -20,8 +20,9 @@
 NB = N * T // B
 PAD = 8
 ROWS = N * CH
-WA = 384
-WB = ROWS - WA
+WA = 256
+WB = 512
+WC = (ROWS - WA - WB) // 2
 KINDS = 6
 MIXED, UP, TAPS, CONV, BACK, FILT = range(KINDS)
 
@@ -104,6 +105,11 @@
     second_out_b,
     third_in_a,
     third_in_b,
+    part_c,
+    across_in,
+    first_in_c,
+    first_out_c,
+    second_in_c,
     send_sem,
     recv_sem,
     x_send_sem,
@@ -273,6 +279,9 @@
     mixed_all[:PAD] = jnp.zeros((PAD, CH, B), BF16)
     up_all[NB:] = jnp.zeros((PAD, CH, B), BF16)
 
+    for_peers(me, lambda peer: mixed_copy(peer).wait_send())
+    for_peers(me, lambda peer: up_copy(peer).start())
+
     wait_all(TAPS, lambda peer: taps_all.at[peer], taps_send.at[0])
     row_id = lax.broadcasted_iota(jnp.int32, (B, B), 0)
     col_id = lax.broadcasted_iota(jnp.int32, (B, B), 1)
@@ -293,9 +302,6 @@
             acc[:B] = now
 
     loop(N, make_tiles)
-
-    for_peers(me, lambda peer: mixed_copy(peer).wait_send())
-    for_peers(me, lambda peer: up_copy(peer).start())
 
     wait_all(MIXED, lambda peer: mixed_all.at[pl.ds(PAD + 2 * peer, 2)], mixed_send.at[:, :CH, :])
 
@@ -393,6 +399,13 @@
         lhs = jnp.concatenate([x_all[16 * pair + 8 * e + 4 * pz + py] for e in range(2)], axis=0)
         part_b[py, pz, pl.ds(2 * pair, 2)] = share(lhs, WA, WB).reshape(2, 128, WB)
 
+    def share_c(pz, px):
+        lhs = x_all[pl.ds(8 * px + 4 * pz, 4)].reshape(512, T)
+        both = share(lhs, WA + WB, 2 * WC)
+        part_c[0, pz, px] = both[:, :WC].reshape(4, 128, WC)
+        for py in range(4):
+            part_c[1, pz, py, px] = both[py * 128 : (py + 1) * 128, WC:]
+
     def x_peer(d):
         return lax.rem(ix + d, 4) * 8 + iz * 4 + iy
 
@@ -465,6 +478,65 @@
     copies_b0 = ring_copies(1, *ring_b0, y_peer)
     copies_b1 = ring_copies(2, *ring_b1, y_peer)
 
+    other = ix * 8 + (1 - iz) * 4 + iy
+
+    def z_copy(slot, held, inbox):
+        return pltpu.make_async_remote_copy(
+            src_ref=held.at[1 - iz],
+            dst_ref=inbox,
+            send_sem=z_send_sem.at[slot],
+            recv_sem=z_recv_sem.at[slot],
+            device_id={"seq": other},
+            device_id_type=MESH,
+        )
+
+    across = [z_copy(2 + c, part_c.at[c], across_in.at[c]) for c in range(2)]
+
+    def view_c(c):
+        return lambda target, side: part_c.at[c, iz, target, pl.ds(2 * side, 2)]
+
+    def second_c(c):
+        return lambda target, side: first_out_c.at[c, target, side]
+
+    rings_c = (
+        (view_c(0), first_in_c.at[0], ix),
+        (view_c(1), first_in_c.at[1], iy),
+    )
+    rings_e = (
+        (second_c(0), second_in_c.at[0], iy),
+        (second_c(1), second_in_c.at[1], ix),
+    )
+    peers_c = (x_peer, y_peer)
+    first_c = [ring_copies(5 + c, *rings_c[c], peers_c[c]) for c in range(2)]
+    last_c = [ring_copies(7 + c, *rings_e[c], peers_c[1 - c]) for c in range(2)]
+
+    def merge_c(c):
+        across[c].wait_recv()
+
+        def add(d):
+            total = part_c[c, iz, d].astype(F32) + across_in[c, d].astype(F32)
+            part_c[c, iz, d] = total.astype(BF16)
+
+        loop(4, add)
+        ring_start(first_c[c])
+
+    def store_c(c):
+        def store(side, e, total):
+            first_out_c[c, 2 * side + e, 0, 0] = total[:64].astype(BF16)
+            first_out_c[c, 2 * side + e, 1, 0] = total[64:].astype(BF16)
+
+        return store
+
+    def final_c(c):
+        def store(side, e, total):
+            first = WA + WB + c * WC
+            rows = slice(64 * side, 64 * side + 64)
+            weight_grad_ref[rows, first : first + WC] = total * weight_factor
+
+        return store
+
+    weight_factor = 1.0 / math.sqrt(N * T)
+
     def shares_b(copies, pair):
         loop(2, lambda z: share_b(lax.rem(iy + 2, 4), z, pair))
         ring_start(copies, 0, 2)
@@ -506,6 +578,9 @@
     filter_some(7)
     filter_some(6)
     x_pass.wait_recv()
+    loop(4, lambda px: share_c(1 - iz, px))
+    across[0].start()
+    across[1].start()
     loop(2, lambda z: share_a(lax.rem(ix + 2, 4), z))
     ring_start(copies_a, 0, 2)
     loop(2, lambda z: share_a(lax.rem(ix + 3 - 2 * z, 4), z))
@@ -516,11 +591,14 @@
     back_all[:, chan_rows(me), :] = back_send[pl.ds(2 * me, 2)]
     loop(2, lambda z: share_a(ix, z))
     loop(2, lambda z: share_b(iy, z, there))
+    loop(4, lambda px: share_c(iz, px))
     filter_some(1)
     ring_middle(copies_a, *ring_a, 4)
     ring_middle(copies_b1, *ring_b1, 2)
     for i in range(2, 6):
         filter_some(i)
+    merge_c(0)
+    merge_c(1)
 
     filt_part[1, NB] = jnp.zeros((8, B), F32)
     taps_factor = 1.0 / math.sqrt(GROUP * N * T)
@@ -568,6 +646,8 @@
 
         return store
 
+    for c in range(2):
+        ring_middle(first_c[c], *rings_c[c], 2)
     ring_end(copies_b0, *ring_b0, 2, store_b(here))
     ring_end(copies_b1, *ring_b1, 2, store_b(there))
     ring_start(copies_d)
@@ -575,24 +655,15 @@
     ring_start(copies_c)
     ring_middle(copies_d, *ring_d, 1)
     ring_middle(copies_c, *ring_c, 1)
+    for c in range(2):
+        ring_end(first_c[c], *rings_c[c], 2, store_c(c))
+        ring_start(last_c[c])
 
     wait_all(FILT, lambda peer: filt_all.at[peer], filt_send.at[0])
     for g in range(2):
         total = jnp.sum(filt_all[16 * g : 16 * g + 16], axis=0)
         for c in range(4):
             filter_grad_ref[g : g + 1, c * 128 : (c + 1) * 128] = total[c : c + 1, :]
-
-    other = ix * 8 + (1 - iz) * 4 + iy
-
-    def z_copy(slot, held, inbox):
-        return pltpu.make_async_remote_copy(
-            src_ref=held.at[1 - iz],
-            dst_ref=inbox,
-            send_sem=z_send_sem.at[slot],
-            recv_sem=z_recv_sem.at[slot],
-            device_id={"seq": other},
-            device_id_type=MESH,
-        )
 
     def keep(held):
         def store(side, e, total):
@@ -606,10 +677,13 @@
     copy_b.start()
     ring_end(copies_c, *ring_c, 1, keep(second_out_a))
     copy_a.start()
-    weight_factor = 1.0 / math.sqrt(N * T)
+    for c in range(2):
+        ring_middle(last_c[c], *rings_e[c], 1)
+    for c in range(2):
+        ring_end(last_c[c], *rings_e[c], 1, final_c(c))
     copy_b.wait_recv()
     total = second_out_b[iz].astype(F32) + third_in_b[...].astype(F32)
-    weight_grad_ref[:, WA:] = total * weight_factor
+    weight_grad_ref[:, WA : WA + WB] = total * weight_factor
     copy_a.wait_recv()
     total = second_out_a[iz].astype(F32) + third_in_a[...].astype(F32)
     weight_grad_ref[:, :WA] = total * weight_factor
@@ -619,6 +693,7 @@
     for make in (taps_copy, up_copy, conv_copy, back_copy, filt_copy):
         for_peers(me, lambda peer: make(peer).wait_send())
     rings = (*copies_a, *copies_b0, *copies_b1, *copies_c, *copies_d)
+    rings += (*first_c[0], *first_c[1], *last_c[0], *last_c[1], *across)
     for c in (x_core, x_near, x_pass, *rings, copy_a, copy_b):
         c.wait_send()
 
@@ -686,14 +761,19 @@
             pltpu.VMEM((2, 128, WB), BF16),
             pltpu.VMEM((128, WA), BF16),
             pltpu.VMEM((128, WB), BF16),
+            pltpu.VMEM((2, 2, 4, 4, 128, WC), BF16),
+            pltpu.VMEM((2, 4, 4, 128, WC), BF16),
+            pltpu.VMEM((2, 6, 2, 128, WC), BF16),
+            pltpu.VMEM((2, 4, 2, 1, 64, WC), BF16),
+            pltpu.VMEM((2, 6, 1, 64, WC), BF16),
             pltpu.SemaphoreType.DMA((KINDS, N)),
             pltpu.SemaphoreType.DMA((KINDS, N)),
             pltpu.SemaphoreType.DMA((3,)),
             pltpu.SemaphoreType.DMA((3,)),
-            pltpu.SemaphoreType.DMA((5, 6)),
-            pltpu.SemaphoreType.DMA((5, 6)),
-            pltpu.SemaphoreType.DMA((2,)),
-            pltpu.SemaphoreType.DMA((2,)),
+            pltpu.SemaphoreType.DMA((9, 6)),
+            pltpu.SemaphoreType.DMA((9, 6)),
+            pltpu.SemaphoreType.DMA((4,)),
+            pltpu.SemaphoreType.DMA((4,)),
             pltpu.SemaphoreType.DMA((5,)),
             pltpu.SemaphoreType.DMA((4,)),
         ],

time: 147 us -> 148 us (level)
  Pallas kernels: 145 us -> 147 us
    pallas_call x1, Pallas kernels: 141 us -> 143 us  [per_device(): pl.pallas_call(kernel, out_shape=shapes, in_specs=[hbm] * 4 + [vmem, hbm]...]
where the time goes in v6:
time: 148 us
  Pallas kernels  147 us (99%)
    pallas_call x1, Pallas kernels, per_device(): pl.pallas_call(kernel, out_shape=shapes, in_specs=[hbm] * 4 + [vmem, hbm]...  143 us
    pallas_call x1, Pallas kernels, per_device(): pl.pallas_call(hand_over, out_shape=shapes, in_specs=[hbm] * 6, out_specs...  3.66 us

profile of v6, /device:TPU:0, one launch (start us, length us, event | category | flops | bytes accessed | tf_op | source)
XLA Modules:
  0.0 147.8 jit_solution(6551770876099844047)
XLA Ops:
  0.6 143.5 %shard_map.109 = (bf16[1024,512]{1,0:T(8,128)(2,1)}, bf16[1024,512]{1,0:T(8,128)(2,1)}, bf16[1024,512]{1,0:T(8,128)(2,1)}, bf16[1024,512]{1,0:T(8,128)(2,1)}, f32[2,512]{1,0:T(2,128)}, /*index=5*/f32[128,1024]{1,0:T(8,128)}) custom-call(bf16[8,128,512]{2,1,0:T(8,128)(2,1)} %bitcast.1, bf16[1024,512]{1,0:T(8,128)(2,1)} %q_hbm.1, bf16[1024,512]{1,0:T(8,128)(2,1)} %k_hbm.1, ...), custom_call_target="tpu_custom_call" | custom-call | tf_op jit(solution)/shard_map/pallas_call | solution.py:728
  144.1 3.7 %shard_map.110 = (bf16[1024,512]{1,0:T(8,128)(2,1)}, bf16[1024,512]{1,0:T(8,128)(2,1)}, bf16[1024,512]{1,0:T(8,128)(2,1)}, bf16[1024,512]{1,0:T(8,128)(2,1)}, f32[2,512]{1,0:T(2,128)}, /*index=5*/f32[128,1024]{1,0:T(8,128)}) custom-call(bf16[1024,512]{1,0:T(8,128)(2,1)} %get-tuple-element.12.refs_0_, bf16[1024,512]{1,0:T(8,128)(2,1)} %get-tuple-element.13.refs_1_, ...), custom_call_target="tpu_custom_call" | custom-call | tf_op jit(solution)/shard_map/pallas_call | solution.py:792

commit v7 on v4

--- a/solution.py
+++ b/solution.py
@@ -362,6 +362,8 @@
     loop(4, back_chunk)
 
     wait_all(CONV, lambda peer: conv_all.at[:, chan_rows(peer), :], conv_send.at[:2])
+    for_peers(me, lambda peer: back_copy(peer).start())
+    back_all[:, chan_rows(me), :] = back_send[pl.ds(2 * me, 2)]
 
     def use_conv(r):
         rows = pl.ds(pl.multiple_of(r * 128, 128), 128)
@@ -498,8 +500,6 @@
     def filter_some(i):
         loop(8, lambda u: filter_tile(i, 8 * i + u))
 
-    filter_some(0)
-    ring_middle(copies_b0, *ring_b0, 2)
 
     x_near.wait_recv()
     x_pass.start()
@@ -512,14 +512,14 @@
     ring_start(copies_a, 2, 4)
     loop(2, lambda z: share_a(lax.rem(ix + 1 + 2 * z, 4), z))
     shares_b(copies_b1, there)
-    for_peers(me, lambda peer: back_copy(peer).start())
-    back_all[:, chan_rows(me), :] = back_send[pl.ds(2 * me, 2)]
     loop(2, lambda z: share_a(ix, z))
     loop(2, lambda z: share_b(iy, z, there))
-    filter_some(1)
+    ring_middle(copies_b0, *ring_b0, 2)
+    filter_some(0)
+    filter_some(4)
     ring_middle(copies_a, *ring_a, 4)
     ring_middle(copies_b1, *ring_b1, 2)
-    for i in range(2, 6):
+    for i in (1, 2, 3, 5):
         filter_some(i)
 
     filt_part[1, NB] = jnp.zeros((8, B), F32)

time: 147 us -> 153 us (1.041)
  Pallas kernels: 145 us -> 152 us
    pallas_call x1, Pallas kernels: 141 us -> 149 us  [per_device(): pl.pallas_call(kernel, out_shape=shapes, in_specs=[hbm] * 4 + [vmem, hbm]...]
where the time goes in v7:
time: 153 us
  Pallas kernels  152 us (99%)
    pallas_call x1, Pallas kernels, per_device(): pl.pallas_call(kernel, out_shape=shapes, in_specs=[hbm] * 4 + [vmem, hbm]...  149 us
    pallas_call x1, Pallas kernels, per_device(): pl.pallas_call(hand_over, out_shape=shapes, in_specs=[hbm] * 6, out_specs...  3.66 us

profile of v7, /device:TPU:0, one launch (start us, length us, event | category | flops | bytes accessed | tf_op | source)
XLA Modules:
  0.0 152.9 jit_solution(675903351659467114)
XLA Ops:
  0.6 148.6 %shard_map.109 = (bf16[1024,512]{1,0:T(8,128)(2,1)}, bf16[1024,512]{1,0:T(8,128)(2,1)}, bf16[1024,512]{1,0:T(8,128)(2,1)}, bf16[1024,512]{1,0:T(8,128)(2,1)}, f32[2,512]{1,0:T(2,128)}, /*index=5*/f32[128,1024]{1,0:T(8,128)}) custom-call(bf16[8,128,512]{2,1,0:T(8,128)(2,1)} %bitcast.1, bf16[1024,512]{1,0:T(8,128)(2,1)} %q_hbm.1, bf16[1024,512]{1,0:T(8,128)(2,1)} %k_hbm.1, ...), custom_call_target="tpu_custom_call" | custom-call | tf_op jit(solution)/shard_map/pallas_call | solution.py:653
  149.3 3.7 %shard_map.110 = (bf16[1024,512]{1,0:T(8,128)(2,1)}, bf16[1024,512]{1,0:T(8,128)(2,1)}, bf16[1024,512]{1,0:T(8,128)(2,1)}, bf16[1024,512]{1,0:T(8,128)(2,1)}, f32[2,512]{1,0:T(2,128)}, /*index=5*/f32[128,1024]{1,0:T(8,128)}) custom-call(bf16[1024,512]{1,0:T(8,128)(2,1)} %get-tuple-element.12.refs_0_, bf16[1024,512]{1,0:T(8,128)(2,1)} %get-tuple-element.13.refs_1_, ...), custom_call_target="tpu_custom_call" | custom-call | tf_op jit(solution)/shard_map/pallas_call | solution.py:712

commit v8 on v6

--- a/solution.py
+++ b/solution.py
@@ -615,6 +615,30 @@
     for_peers(me, lambda peer: filt_copy(peer).start())
     filt_all[me] = filt_send[me]
 
+    def second_view(held):
+        return lambda target, side: held.at[target, side]
+
+    ring_c = (second_view(first_out_a), second_in_a, iy)
+    ring_d = (second_view(first_out_b), second_in_b, ix)
+    copies_c = ring_copies(3, *ring_c, y_peer)
+    copies_d = ring_copies(4, *ring_d, x_peer)
+
+    def store_a(side, e, total):
+        first_out_a[e, side, 0] = total.astype(BF16)
+
+    def store_b(pair):
+        def store(side, e, total):
+            first_out_b[2 * pair + e, side, 0] = total.astype(BF16)
+
+        return store
+
+    ring_end(copies_b0, *ring_b0, 2, store_b(here))
+    ring_end(copies_b1, *ring_b1, 2, store_b(there))
+    ring_start(copies_d)
+    ring_end(copies_a, *ring_a, 4, store_a)
+    ring_start(copies_c)
+    for c in range(2):
+        ring_middle(first_c[c], *rings_c[c], 2)
     wait_all(BACK, lambda peer: back_all.at[:, chan_rows(peer), :], back_send.at[:2])
 
     def use_back(r):
@@ -629,30 +653,6 @@
     stores[2].start()
     stores[3].start()
 
-    def second_view(held):
-        return lambda target, side: held.at[target, side]
-
-    ring_c = (second_view(first_out_a), second_in_a, iy)
-    ring_d = (second_view(first_out_b), second_in_b, ix)
-    copies_c = ring_copies(3, *ring_c, y_peer)
-    copies_d = ring_copies(4, *ring_d, x_peer)
-
-    def store_a(side, e, total):
-        first_out_a[e, side, 0] = total.astype(BF16)
-
-    def store_b(pair):
-        def store(side, e, total):
-            first_out_b[2 * pair + e, side, 0] = total.astype(BF16)
-
-        return store
-
-    for c in range(2):
-        ring_middle(first_c[c], *rings_c[c], 2)
-    ring_end(copies_b0, *ring_b0, 2, store_b(here))
-    ring_end(copies_b1, *ring_b1, 2, store_b(there))
-    ring_start(copies_d)
-    ring_end(copies_a, *ring_a, 4, store_a)
-    ring_start(copies_c)
     ring_middle(copies_d, *ring_d, 1)
     ring_middle(copies_c, *ring_c, 1)
     for c in range(2):

time: 148 us -> 145 us (0.980)
  Pallas kernels: 147 us -> 144 us
    pallas_call x1, Pallas kernels: 143 us -> 141 us  [per_device(): pl.pallas_call(kernel, out_shape=shapes, in_specs=[hbm] * 4 + [vmem, hbm]...]
where the time goes in v8:
time: 145 us
  Pallas kernels  144 us (99%)
    pallas_call x1, Pallas kernels, per_device(): pl.pallas_call(kernel, out_shape=shapes, in_specs=[hbm] * 4 + [vmem, hbm]...  141 us
    pallas_call x1, Pallas kernels, per_device(): pl.pallas_call(hand_over, out_shape=shapes, in_specs=[hbm] * 6, out_specs...  3.66 us

profile of v8, /device:TPU:0, one launch (start us, length us, event | category | flops | bytes accessed | tf_op | source)
XLA Modules:
  0.0 145.0 jit_solution(614865316820141799)
XLA Ops:
  0.6 140.7 %shard_map.109 = (bf16[1024,512]{1,0:T(8,128)(2,1)}, bf16[1024,512]{1,0:T(8,128)(2,1)}, bf16[1024,512]{1,0:T(8,128)(2,1)}, bf16[1024,512]{1,0:T(8,128)(2,1)}, f32[2,512]{1,0:T(2,128)}, /*index=5*/f32[128,1024]{1,0:T(8,128)}) custom-call(bf16[8,128,512]{2,1,0:T(8,128)(2,1)} %bitcast.1, bf16[1024,512]{1,0:T(8,128)(2,1)} %q_hbm.1, bf16[1024,512]{1,0:T(8,128)(2,1)} %k_hbm.1, ...), custom_call_target="tpu_custom_call" | custom-call | tf_op jit(solution)/shard_map/pallas_call | solution.py:728
  141.3 3.7 %shard_map.110 = (bf16[1024,512]{1,0:T(8,128)(2,1)}, bf16[1024,512]{1,0:T(8,128)(2,1)}, bf16[1024,512]{1,0:T(8,128)(2,1)}, bf16[1024,512]{1,0:T(8,128)(2,1)}, f32[2,512]{1,0:T(2,128)}, /*index=5*/f32[128,1024]{1,0:T(8,128)}) custom-call(bf16[1024,512]{1,0:T(8,128)(2,1)} %get-tuple-element.12.refs_0_, bf16[1024,512]{1,0:T(8,128)(2,1)} %get-tuple-element.13.refs_1_, ...), custom_call_target="tpu_custom_call" | custom-call | tf_op jit(solution)/shard_map/pallas_call | solution.py:792

commit v9 on v8

--- a/solution.py
+++ b/solution.py
@@ -587,14 +587,14 @@
     ring_start(copies_a, 2, 4)
     loop(2, lambda z: share_a(lax.rem(ix + 1 + 2 * z, 4), z))
     shares_b(copies_b1, there)
-    for_peers(me, lambda peer: back_copy(peer).start())
-    back_all[:, chan_rows(me), :] = back_send[pl.ds(2 * me, 2)]
     loop(2, lambda z: share_a(ix, z))
     loop(2, lambda z: share_b(iy, z, there))
     loop(4, lambda px: share_c(iz, px))
     filter_some(1)
     ring_middle(copies_a, *ring_a, 4)
     ring_middle(copies_b1, *ring_b1, 2)
+    for_peers(me, lambda peer: back_copy(peer).start())
+    back_all[:, chan_rows(me), :] = back_send[pl.ds(2 * me, 2)]
     for i in range(2, 6):
         filter_some(i)
     merge_c(0)
@@ -639,6 +639,31 @@
     ring_start(copies_c)
     for c in range(2):
         ring_middle(first_c[c], *rings_c[c], 2)
+    ring_middle(copies_d, *ring_d, 1)
+    ring_middle(copies_c, *ring_c, 1)
+    for c in range(2):
+        ring_end(first_c[c], *rings_c[c], 2, store_c(c))
+        ring_start(last_c[c])
+
+    wait_all(FILT, lambda peer: filt_all.at[peer], filt_send.at[0])
+    for g in range(2):
+        total = jnp.sum(filt_all[16 * g : 16 * g + 16], axis=0)
+        for c in range(4):
+            filter_grad_ref[g : g + 1, c * 128 : (c + 1) * 128] = total[c : c + 1, :]
+
+    def keep(held):
+        def store(side, e, total):
+            held[side] = total.astype(BF16)
+
+        return store
+
+    copy_b = z_copy(1, second_out_b, third_in_b)
+    copy_a = z_copy(0, second_out_a, third_in_a)
+    ring_end(copies_d, *ring_d, 1, keep(second_out_b))
+    copy_b.start()
+    ring_end(copies_c, *ring_c, 1, keep(second_out_a))
+    copy_a.start()
+
     wait_all(BACK, lambda peer: back_all.at[:, chan_rows(peer), :], back_send.at[:2])
 
     def use_back(r):
@@ -653,30 +678,6 @@
     stores[2].start()
     stores[3].start()
 
-    ring_middle(copies_d, *ring_d, 1)
-    ring_middle(copies_c, *ring_c, 1)
-    for c in range(2):
-        ring_end(first_c[c], *rings_c[c], 2, store_c(c))
-        ring_start(last_c[c])
-
-    wait_all(FILT, lambda peer: filt_all.at[peer], filt_send.at[0])
-    for g in range(2):
-        total = jnp.sum(filt_all[16 * g : 16 * g + 16], axis=0)
-        for c in range(4):
-            filter_grad_ref[g : g + 1, c * 128 : (c + 1) * 128] = total[c : c + 1, :]
-
-    def keep(held):
-        def store(side, e, total):
-            held[side] = total.astype(BF16)
-
-        return store
-
-    copy_b = z_copy(1, second_out_b, third_in_b)
-    copy_a = z_copy(0, second_out_a, third_in_a)
-    ring_end(copies_d, *ring_d, 1, keep(second_out_b))
-    copy_b.start()
-    ring_end(copies_c, *ring_c, 1, keep(second_out_a))
-    copy_a.start()
     for c in range(2):
         ring_middle(last_c[c], *rings_e[c], 1)
     for c in range(2):

time: 145 us -> 146 us (level)
  no operation moved by 1% of the time
where the time goes in v9:
time: 146 us; the launch traced here: 145 us
  Pallas kernels  145 us (99%)
    pallas_call x1, Pallas kernels, per_device(): pl.pallas_call(kernel, out_shape=shapes, in_specs=[hbm] * 4 + [vmem, hbm]...  141 us
    pallas_call x1, Pallas kernels, per_device(): pl.pallas_call(hand_over, out_shape=shapes, in_specs=[hbm] * 6, out_specs...  3.66 us

profile of v9, /device:TPU:0, one launch (start us, length us, event | category | flops | bytes accessed | tf_op | source)
XLA Modules:
  0.0 145.4 jit_solution(9165116710758137730)
XLA Ops:
  0.6 141.1 %shard_map.109 = (bf16[1024,512]{1,0:T(8,128)(2,1)}, bf16[1024,512]{1,0:T(8,128)(2,1)}, bf16[1024,512]{1,0:T(8,128)(2,1)}, bf16[1024,512]{1,0:T(8,128)(2,1)}, f32[2,512]{1,0:T(2,128)}, /*index=5*/f32[128,1024]{1,0:T(8,128)}) custom-call(bf16[8,128,512]{2,1,0:T(8,128)(2,1)} %bitcast.1, bf16[1024,512]{1,0:T(8,128)(2,1)} %q_hbm.1, bf16[1024,512]{1,0:T(8,128)(2,1)} %k_hbm.1, ...), custom_call_target="tpu_custom_call" | custom-call | tf_op jit(solution)/shard_map/pallas_call | solution.py:729
  141.7 3.7 %shard_map.110 = (bf16[1024,512]{1,0:T(8,128)(2,1)}, bf16[1024,512]{1,0:T(8,128)(2,1)}, bf16[1024,512]{1,0:T(8,128)(2,1)}, bf16[1024,512]{1,0:T(8,128)(2,1)}, f32[2,512]{1,0:T(2,128)}, /*index=5*/f32[128,1024]{1,0:T(8,128)}) custom-call(bf16[1024,512]{1,0:T(8,128)(2,1)} %get-tuple-element.12.refs_0_, bf16[1024,512]{1,0:T(8,128)(2,1)} %get-tuple-element.13.refs_1_, ...), custom_call_target="tpu_custom_call" | custom-call | tf_op jit(solution)/shard_map/pallas_call | solution.py:793
